TPU v7x, 512 devices: a whole 4x8x8 slice. The times are simulated.
512 devices in a mesh: vtx: 64 (over z, y), pose: 8 (over x, core).
Axes of the slice: x: 4, y: 8, z: 8, core: 2. Of those that a mesh axis runs over, the one named last changes fastest.
Arguments:
- skin_weights: bfloat16 [524288, 128], P('vtx'), may hold values from -1.1 to 1.1
- bone_ids: int32 [2048, 4], P('vtx'), may hold values from 0 to 127, as said below
- slot_mask: int32 [2048, 4], P('vtx'), may hold values 0 or 1
- pose_coeffs: bfloat16 [128, 32, 2048], P(None, None, 'pose'), may hold values from -9 to 9
Outputs:
- projected: bfloat16 [524288, 2048], P('vtx', 'pose')
Inputs may be any that keep to these rules, and one draw needn't show every extreme that they name: `bone_ids`: the 4 bone ids of a block are distinct.
All inputs are finite; a program needn't handle non-finite values. No bound on the sum of `slot_mask` on one device may be relied on, other than what follows from the above.
Results may differ from a plain program's by a relative error of at most 0.012.
Values may be sent and summed in bfloat16 or wider, within the bound.
A program may use at most 64 MiB of HBM per device.

v0:
```python
import jax
import jax.numpy as jnp
from jax import lax
from jax.sharding import PartitionSpec as P

RANK = 64
SWEEPS = 3


def partner_2(value, axis, apart):
    mask = 2**apart
    pairs = [(source, source ^ mask) for source in range(lax.axis_size(axis))]
    return lax.ppermute(value, axis, pairs)


def orthonormal(columns):
    cross_gram = jnp.dot(
        columns.T, columns, precision=lax.Precision.HIGHEST, preferred_element_type=jnp.float32
    )
    lower_factor = jnp.linalg.cholesky(cross_gram)
    return jax.scipy.linalg.solve_triangular(lower_factor, columns.T, lower=True).T


def top_space(gram_matrix):
    columns = orthonormal(gram_matrix[:, :RANK])
    for sweep_index in range(SWEEPS - 1):
        columns = orthonormal(
            jnp.dot(
                gram_matrix,
                columns,
                precision=lax.Precision.HIGHEST,
                preferred_element_type=jnp.float32,
            )
        )
    return columns


def merge_rows(joined, gram_matrix):
    return jnp.dot(
        joined,
        top_space(gram_matrix),
        precision=lax.Precision.HIGHEST,
        preferred_element_type=jnp.float32,
    )


def per_device(skin_weights, bone_ids, slot_mask, pose_coeffs):
    block_count = bone_ids.shape[0]
    row_count = skin_weights.shape[0]
    block_rows = row_count // block_count
    chosen = jnp.take(pose_coeffs, bone_ids, axis=0) * slot_mask[:, :, None, None].astype(
        jnp.bfloat16
    )
    chosen = chosen.reshape(block_count, skin_weights.shape[1], -1)
    row_blocks = skin_weights.reshape(block_count, block_rows, -1)
    slab_shard = jnp.einsum("brk,bkp->brp", row_blocks, chosen, preferred_element_type=jnp.float32)
    slab_shard = slab_shard.astype(jnp.bfloat16).reshape(row_count, -1)
    leaf_matrix = lax.psum(
        jnp.dot(slab_shard.T, slab_shard, preferred_element_type=jnp.float32), "vtx"
    )
    rotation = top_space(leaf_matrix).astype(jnp.bfloat16)
    sketch = jnp.dot(slab_shard, rotation, preferred_element_type=jnp.float32)
    levels = lax.axis_size("pose").bit_length() - 1
    position = lax.axis_index("pose")
    for level_index in range(levels):
        partner = partner_2(sketch, "pose", level_index)
        upper_half = position // 2**level_index % 2 == 1
        joined = jnp.where(
            upper_half,
            jnp.concatenate([partner, sketch], axis=1),
            jnp.concatenate([sketch, partner], axis=1),
        )
        partial_gram = jnp.dot(
            joined.T, joined, precision=lax.Precision.HIGHEST, preferred_element_type=jnp.float32
        )
        gram_matrix = lax.psum(partial_gram, "vtx")
        sketch = merge_rows(joined, gram_matrix)
    basis_rows = sketch.astype(jnp.bfloat16)
    cross_gram, moments = lax.psum(
        (
            jnp.dot(basis_rows.T, basis_rows, preferred_element_type=jnp.float32),
            jnp.dot(basis_rows.T, slab_shard, preferred_element_type=jnp.float32),
        ),
        "vtx",
    )
    lower_factor = jnp.linalg.cholesky(cross_gram)
    coefficients = jax.scipy.linalg.cho_solve((lower_factor, True), moments).astype(jnp.bfloat16)
    return jnp.dot(basis_rows, coefficients, preferred_element_type=jnp.float32).astype(
        jnp.bfloat16
    )


def solution(mesh):
    in_specs = (P("vtx", None), P("vtx", None), P("vtx", None), P(None, None, "pose"))
    out_specs = P("vtx", "pose")
    return jax.shard_map(
        per_device, mesh=mesh, in_specs=in_specs, out_specs=out_specs, check_vma=False
    )
```

profile of v0, /device:TPU:2, one launch (start us, length us, event | category | flops | bytes accessed | tf_op | source)
XLA Modules:
  0.0 1239.0 jit_solution(12157800520885964022)
XLA Ops:
  21.7 156.7 %all-reduce.6.cloned.1.call-done = f32[256,256]{1,0:T(8,128)} async-done(((f32[256,256]{1,0:T(8,128)}), f32[256,256]{1,0:T(8,128)}) %all-reduce.6.cloned.1.call-update) | async-done | bytes 262160 | tf_op jit(solution)/shard_map/psum | solution.py:58
  179.8 5.8 cholesky.209
  194.8 5.8 cholesky.220
  208.8 5.8 cholesky.231
  232.6 10.8 fusion.6
  243.4 145.5 %all-reduce.8.cloned.1.call-done = f32[128,128]{1,0:T(8,128)} async-done(((f32[128,128]{1,0:T(8,128)}), f32[128,128]{1,0:T(8,128)}) %all-reduce.8.cloned.1.call-update) | async-done | bytes 65552 | tf_op jit(solution)/shard_map/psum | solution.py:76
  390.2 5.8 cholesky.242
  404.8 5.8 cholesky.253
  418.5 5.8 cholesky.264
  430.9 7.4 fusion.5
  438.4 11.8 collective-permute-start.1
  450.2 33.1 %collective-permute-done.1 = f32[8192,64]{0,1:T(8,128)} collective-permute-done((f32[8192,64]{0,1:T(8,128)}, f32[8192,64]{0,1:T(8,128)}, u32[]{:S(2)}, u32[]{:S(2)}) %collective-permute-start.1) | collective-permute-done | bytes 2097184 | tf_op jit(solution)/shard_map/ppermute | solution.py:13
  483.3 10.3 fusion.4
  493.7 144.5 %all-reduce.10.cloned.1.call-done = f32[128,128]{1,0:T(8,128)} async-done(((f32[128,128]{1,0:T(8,128)}), f32[128,128]{1,0:T(8,128)}) %all-reduce.10.cloned.1.call-update) | async-done | bytes 65552 | tf_op jit(solution)/shard_map/psum | solution.py:76
  639.5 5.8 cholesky.275
  654.1 5.8 cholesky.286
  667.9 5.8 cholesky.297
  680.2 7.4 fusion.3
  691.8 42.2 %collective-permute-done.2 = f32[8192,64]{0,1:T(8,128)} collective-permute-done((f32[8192,64]{0,1:T(8,128)}, f32[8192,64]{0,1:T(8,128)}, u32[]{:S(2)}, u32[]{:S(2)}) %collective-permute-start.2) | collective-permute-done | bytes 2097184 | tf_op jit(solution)/shard_map/ppermute | solution.py:13
  734.0 10.5 fusion.2
  744.6 144.6 %all-reduce.12.cloned.1.call-done = f32[128,128]{1,0:T(8,128)} async-done(((f32[128,128]{1,0:T(8,128)}), f32[128,128]{1,0:T(8,128)}) %all-reduce.12.cloned.1.call-update) | async-done | bytes 65552 | tf_op jit(solution)/shard_map/psum | solution.py:76
  890.4 5.8 cholesky.308
  930.9 6.2 convolution_convert_fusion.1
  939.0 276.3 %psum.46 = f32[64,64]{0,1:T(8,128)S(1)} all-reduce(f32[64,64]{0,1:T(8,128)S(1)} %fusion.120), channel_id=1, replica_groups=mesh['vtx'=64,'pose'=8] {'vtx'}, use_global_device_ids=true, to_apply=%region_6.10 | all-reduce | flops 4096 | bytes 32768 | tf_op jit(solution)/shard_map/psum | solution.py:79
  (155 shorter events, 158.9 us)
Async XLA Ops:
  6.5 9.8 copy-start
  6.5 171.8 %all-reduce.6.cloned.1.call-start = ((), (), s32[]{:S(2)}) async-start(), calls=%async_computation | async-start | bytes 524288 | tf_op jit(solution)/shard_map/psum | solution.py:58
  17.6 2.0 copy-start.1
  21.6 367.3 %all-reduce.8.cloned.1.call-start = ((), (), s32[]{:S(2)}) async-start(), calls=%async_computation.1 | async-start | bytes 131072 | tf_op jit(solution)/shard_map/psum | solution.py:76
  226.2 6.4 collective-permute-start
  243.4 394.9 %all-reduce.10.cloned.1.call-start = ((), (), s32[]{:S(2)}) async-start(), calls=%async_computation.2 | async-start | bytes 131072 | tf_op jit(solution)/shard_map/psum | solution.py:76
  438.4 45.0 %collective-permute-start.1 = (f32[8192,64]{0,1:T(8,128)}, f32[8192,64]{0,1:T(8,128)}, u32[]{:S(2)}, u32[]{:S(2)}) collective-permute-start(f32[8192,64]{0,1:T(8,128)} %fusion.5), channel_id=1, source_target_pairs={{0,2},{1,3},{2,0},{3,1},{4,6},{5,7},{6,4},{7,5},{8,10},{9,11},{10,... | collective-permute-start | bytes 6291464 | tf_op jit(solution)/shard_map/ppermute | solution.py:13
  493.7 395.5 %all-reduce.12.cloned.1.call-start = ((), (), s32[]{:S(2)}) async-start(), calls=%async_computation.3 | async-start | bytes 131072 | tf_op jit(solution)/shard_map/psum | solution.py:76
  687.5 46.5 %collective-permute-start.2 = (f32[8192,64]{0,1:T(8,128)}, f32[8192,64]{0,1:T(8,128)}, u32[]{:S(2)}, u32[]{:S(2)}) collective-permute-start(f32[8192,64]{0,1:T(8,128)} %fusion.3), channel_id=1, source_target_pairs={{0,4},{1,5},{2,6},{3,7},{4,0},{5,1},{6,2},{7,3},{8,12},{9,13},{10,... | collective-permute-start | bytes 6291464 | tf_op jit(solution)/shard_map/ppermute | solution.py:13
  744.5 482.9 %all-reduce.14.cloned.1.call-start = ((), (), s32[]{:S(2)}) async-start(), calls=%async_computation.4 | async-start | bytes 131072 | tf_op jit(solution)/shard_map/psum | solution.py:79
  930.6 6.5 copy-start.2
Sparse Core Ops, SparseCore 0:
  21.7 156.5 all-reduce.5
  243.5 145.3 all-reduce.7
  493.8 144.4 all-reduce.9
  744.7 144.4 all-reduce.11
  939.1 143.9 all-reduce.13
where the time goes:
time: 1250 us; the launch traced here: 1240 us
  waiting for transfers between devices  671 us (54%)
  blocking collectives  276 us (22%)
  other arithmetic  163 us (13%)
  matrix products  89.3 us (7%)
  starting transfers between devices  18.3 us (1%)
  between operations  14.3 us (1%)
    psum x3, waiting for transfers between devices, per_device(): gram_matrix = lax.psum(partial_gram, 'vtx')  435 us
    psum x1, blocking collectives, per_device(): lax.psum((jnp.dot(basis_rows.T, basis_rows, preferred_element_type=jnp.fl...  276 us
    psum x1, waiting for transfers between devices, per_device(): lax.psum(jnp.dot(slab_shard.T, slab_shard, preferred_element_type=jnp.flo...  157 us
    ppermute x3, waiting for transfers between devices, partner_2(): return lax.ppermute(value, axis, pairs)  79.6 us
    another operation x36, other arithmetic, orthonormal(): lower_factor = jnp.linalg.cholesky(cross_gram)  78.7 us
    another operation x24, other arithmetic, orthonormal(): jax.scipy.linalg.solve_triangular(lower_factor, columns.T, lower=True)  66.3 us
    dot_general x3, matrix products, per_device(): jnp.dot(joined.T, joined, precision=lax.Precision.HIGHEST, preferred_elem...  31.6 us
  transfers between devices with their start and end apart: 8, of which 7 were waited for; matrix products, arithmetic and copies ran while one was open for 1% of the time, Pallas kernels for 0%

commit v1 on v0

v1 whole, which is shorter than its diff:
```python
import functools

import jax
import jax.numpy as jnp
from jax import lax
from jax.experimental import pallas as pl
from jax.experimental.pallas import tpu as pltpu
from jax.sharding import PartitionSpec as P

RANK = 64
SWEEPS = 3
SHAPES = 32
SIDE = 8
F32 = jnp.float32
BF16 = jnp.bfloat16
HIGHEST = lax.Precision.HIGHEST
MESH = pl.DeviceIdType.MESH
VMEM = pl.BlockSpec(memory_space=pltpu.VMEM)
SMEM = pl.BlockSpec(memory_space=pltpu.SMEM)


def dot(a, b, dims, precision=None):
    return lax.dot_general(a, b, (dims, ((), ())), precision=precision, preferred_element_type=F32)


NN = ((1,), (0,))
NT = ((1,), (1,))
TN = ((0,), (0,))


def leaf_kernel(skin_ref, ids_ref, mask_ref, coeffs_ref, gram_ref, image_ref, chosen_ref, sums_ref):
    block_count, slots = ids_ref.shape
    block_rows = skin_ref.shape[0] // block_count
    sums_ref[...] = jnp.zeros_like(sums_ref)
    gram_ref[...] = jnp.zeros_like(gram_ref)

    def step(block, carry):
        for slot in range(slots):
            place = pl.multiple_of(ids_ref[block, slot] * SHAPES, SHAPES)
            values = coeffs_ref[pl.ds(place, SHAPES), :]
            active = mask_ref[block, slot] != 0
            chosen_ref[slot * SHAPES : (slot + 1) * SHAPES, :] = jnp.where(
                active, values, jnp.zeros_like(values)
            )
        rows = skin_ref[pl.ds(pl.multiple_of(block * block_rows, block_rows), block_rows), :]
        slab = dot(rows, chosen_ref[...], NN).astype(BF16)
        gram_ref[...] += dot(slab, slab, TN)
        image = dot(rows, slab, TN)
        for slot in range(slots):
            place = pl.multiple_of(ids_ref[block, slot] * SHAPES, SHAPES)
            active = mask_ref[block, slot] != 0
            values = image[slot * SHAPES : (slot + 1) * SHAPES, :]
            sums_ref[pl.ds(place, SHAPES), :] += jnp.where(active, values, jnp.zeros_like(values))
        return carry

    lax.fori_loop(0, block_count, step, 0)
    image_ref[...] = sums_ref[...].astype(BF16)


def my_place():
    vtx, pose = lax.axis_index("vtx"), lax.axis_index("pose")
    return vtx // SIDE, lax.rem(vtx, SIDE), pose


def vtx_peer(axis, z, y, pose, offset):
    if axis == "y":
        other = lax.rem(y + offset, SIDE)
        return other, (z * SIDE + other, pose)
    other = lax.rem(z + offset, SIDE)
    return other, (other * SIDE + y, pose)


def greet(devices):
    barrier = pltpu.get_barrier_semaphore()
    for device in devices:
        pl.semaphore_signal(barrier, inc=1, device_id=device, device_id_type=MESH)
    pl.semaphore_wait(barrier, len(devices))


def vtx_devices(z, y, pose):
    found = []
    for axis in ("y", "z"):
        for offset in range(1, SIDE):
            found.append(vtx_peer(axis, z, y, pose, offset)[1])
    return found


def exchange(parts, axis_of_half, source_of, target_of, send_sem, recv_sem, place):
    z, y, pose = place
    copies = []
    for half in range(parts):
        axis = axis_of_half[half]
        me = y if axis == "y" else z
        for offset in range(1, SIDE):
            other, device = vtx_peer(axis, z, y, pose, offset)
            copy = pltpu.make_async_remote_copy(
                src_ref=source_of(half, other),
                dst_ref=target_of(half, me),
                send_sem=send_sem.at[half, offset],
                recv_sem=recv_sem.at[half, me],
                device_id=device,
                device_id_type=MESH,
            )
            copy.start()
            copies.append(copy)
    return copies


def arrived(half, axis, target_of, send_sem, recv_sem, place):
    z, y, pose = place
    for offset in range(1, SIDE):
        other, device = vtx_peer(axis, z, y, pose, offset)
        pltpu.make_async_remote_copy(
            src_ref=target_of(half, other),
            dst_ref=target_of(half, other),
            send_sem=send_sem.at[half, offset],
            recv_sem=recv_sem.at[half, other],
            device_id=device,
            device_id_type=MESH,
        ).wait_recv()


def vtx_sum(source, first, second, total, sems, place):
    z, y, pose = place
    outer, inner = ("y", "z"), ("z", "y")
    mine = {"y": y, "z": z}
    sent = exchange(
        2, outer, lambda h, o: source.at[h, o], lambda h, m: first.at[h, m], sems[0], sems[1], place
    )
    for half in range(2):
        arrived(half, outer[half], lambda h, o: first.at[h, o], sems[0], sems[1], place)
        me = mine[outer[half]]
        first[half, me] = source[half, me]
        value = first[half, 0]
        for index in range(1, SIDE):
            value += first[half, index]
        second[half, mine[inner[half]]] = value
        sent += exchange_one(half, inner[half], second, sems[2], sems[3], place)
    for half in range(2):
        arrived(half, inner[half], lambda h, o: second.at[h, o], sems[2], sems[3], place)
        value = second[half, 0]
        for index in range(1, SIDE):
            value += second[half, index]
        total[half, mine[outer[half]]] = value
        sent += exchange_one(half, outer[half], total, sems[4], sems[5], place)
    for half in range(2):
        arrived(half, outer[half], lambda h, o: total.at[h, o], sems[4], sems[5], place)
    for copy in sent:
        copy.wait_send()


def exchange_one(half, axis, buffer, send_sem, recv_sem, place):
    z, y, pose = place
    me = y if axis == "y" else z
    copies = []
    for offset in range(1, SIDE):
        other, device = vtx_peer(axis, z, y, pose, offset)
        copy = pltpu.make_async_remote_copy(
            src_ref=buffer.at[half, me],
            dst_ref=buffer.at[half, me],
            send_sem=send_sem.at[half, offset],
            recv_sem=recv_sem.at[half, me],
            device_id=device,
            device_id_type=MESH,
        )
        copy.start()
        copies.append(copy)
    return copies


def to_chunks(matrix_ref, chunks_ref):
    depth = chunks_ref.shape[2]
    for half in range(2):
        for chunk in range(SIDE):
            chunks_ref[half, chunk] = matrix_ref[
                chunk * depth : (chunk + 1) * depth, half * 128 : (half + 1) * 128
            ]


def from_chunks(chunks_ref, matrix_ref):
    depth = chunks_ref.shape[2]
    for half in range(2):
        for chunk in range(SIDE):
            matrix_ref[chunk * depth : (chunk + 1) * depth, half * 128 : (half + 1) * 128] = chunks_ref[
                half, chunk
            ]


def gram_sum_kernel(part_ref, gram_ref, source, first, second, total, *sems):
    place = my_place()
    to_chunks(part_ref, source)
    greet(vtx_devices(*place))
    vtx_sum(source, first, second, total, sems, place)
    from_chunks(total, gram_ref)


def sum_scratch(rows):
    return [pltpu.VMEM((2, SIDE, rows // SIDE, 128), F32)] * 4 + [
        pltpu.SemaphoreType.DMA((2, SIDE))
    ] * 6


def inverse_factors(grams, identity_part):
    count = len(grams)
    groups = RANK // 8
    rows = [[gram[8 * g : 8 * g + 8] for g in range(groups)] for gram in grams]
    sublane = lax.broadcasted_iota(jnp.int32, (8, 128), 0)
    for n in range(count):
        for g in range(groups):
            rows[n][g] = rows[n][g] + identity_part[8 * g : 8 * g + 8]
    for p in range(groups):
        for n in range(count):
            own = rows[n]
            spread = [
                [
                    jnp.broadcast_to(own[g][:, RANK + 8 * p + c : RANK + 8 * p + c + 1], (8, 128))
                    for g in range(p, groups)
                ]
                for c in range(8)
            ]
            pivots = jnp.ones((8, 128), F32)
            for c in range(8):
                pivot = jnp.broadcast_to(spread[c][0][c : c + 1, :], (8, 128))
                pivots = jnp.where(sublane == c, pivot, pivots)
                inverse = 1.0 / pivot
                lead = jnp.broadcast_to(own[p][c : c + 1, :], (8, 128)) * inverse
                leads = [
                    jnp.broadcast_to(spread[d][0][c : c + 1, :], (8, 128)) * inverse
                    for d in range(c + 1, 8)
                ]
                for g in range(p, groups):
                    column = spread[c][g - p]
                    if g == p:
                        column = jnp.where(sublane > c, column, 0.0)
                    own[g] = own[g] - column * lead
                    for d in range(c + 1, 8):
                        spread[d][g - p] = spread[d][g - p] - column * leads[d - c - 1]
            own[p] = own[p] * lax.rsqrt(pivots)
    return [jnp.concatenate(own, axis=0)[:, :RANK] for own in rows]


def identity_lanes():
    row = lax.broadcasted_iota(jnp.int32, (RANK, 128), 0)
    lane = lax.broadcasted_iota(jnp.int32, (RANK, 128), 1)
    return jnp.where(row == lane, 1.0, 0.0).astype(F32)


def orthonormal(columns, identity_part):
    grams = []
    for value in columns:
        padded = jnp.concatenate([jnp.zeros_like(value), value], axis=0)
        grams.append(dot(value, padded, NT, HIGHEST))
    factors = inverse_factors(grams, identity_part)
    return [dot(factor, value, NN, HIGHEST) for factor, value in zip(factors, columns)]


def top_spaces(grams, identity_part):
    columns = orthonormal([gram[:RANK, :] for gram in grams], identity_part)
    for sweep in range(SWEEPS - 1):
        columns = orthonormal(
            [dot(value, gram, NN, HIGHEST) for value, gram in zip(columns, grams)], identity_part
        )
    return columns


def turn_kernel(gram_ref, coeffs_ref, turn_ref, sketch_ref):
    turn = top_spaces([gram_ref[...]], identity_lanes())[0].astype(BF16)
    turn_ref[...] = turn
    sketch_ref[...] = dot(turn, coeffs_ref[...], NT).astype(BF16)


def joint_kernel(sketch_ref, image_ref, turn_ref, all_ref, product_ref, gram_ref, *scratch):
    partial_ref, source, first, second, total = scratch[:5]
    sems = scratch[5:11]
    send_sem, recv_sem, gram_send, gram_recv = scratch[11:]
    place = my_place()
    z, y, pose = place
    vtx = z * SIDE + y
    poses = all_ref.shape[0]
    chips = poses // 2
    x, core = pose // 2, lax.rem(pose, 2)
    sibling = (vtx, x * 2 + 1 - core)
    pose_devices = [(vtx, lax.rem(pose + offset, poses)) for offset in range(1, poses)]
    greet(vtx_devices(*place) + pose_devices)

    def send(source_ref, slot, device, number):
        copy = pltpu.make_async_remote_copy(
            src_ref=source_ref,
            dst_ref=all_ref.at[slot],
            send_sem=send_sem.at[number],
            recv_sem=recv_sem.at[slot],
            device_id=device,
            device_id_type=MESH,
        )
        copy.start()
        return copy

    def wait_for(slot, device):
        pltpu.make_async_remote_copy(
            src_ref=all_ref.at[slot],
            dst_ref=all_ref.at[slot],
            send_sem=send_sem.at[0],
            recv_sem=recv_sem.at[slot],
            device_id=device,
            device_id_type=MESH,
        ).wait_recv()

    sent = []
    for offset in (1, chips - 1, 2):
        other = lax.rem(x + offset, chips)
        sent.append(send(sketch_ref, pose, (vtx, other * 2 + core), offset))
    sent.append(send(sketch_ref, pose, sibling, 0))
    all_ref[pose] = sketch_ref[...]
    for offset in (1, chips - 1, 2):
        other = lax.rem(x + offset, chips)
        slot = other * 2 + core
        wait_for(slot, (vtx, slot))
        sent.append(send(all_ref.at[slot], slot, sibling, chips + offset))
    for offset in range(chips):
        slot = lax.rem(x + offset, chips) * 2 + 1 - core
        wait_for(slot, sibling)
    for index in range(poses):
        partial_ref[index * RANK : (index + 1) * RANK, :] = dot(all_ref[index], image_ref[...], NN)
    to_chunks(partial_ref, source)
    vtx_sum(source, first, second, total, sems, place)
    from_chunks(total, product_ref)
    gram_ref[pose] = dot(turn_ref[...].astype(F32), product_ref[...], NT, HIGHEST)
    for offset in range(1, poses):
        copy = pltpu.make_async_remote_copy(
            src_ref=gram_ref.at[pose],
            dst_ref=gram_ref.at[pose],
            send_sem=gram_send.at[offset],
            recv_sem=gram_recv.at[pose],
            device_id=(vtx, lax.rem(pose + offset, poses)),
            device_id_type=MESH,
        )
        copy.start()
        sent.append(copy)
    for offset in range(1, poses):
        other = lax.rem(pose + offset, poses)
        pltpu.make_async_remote_copy(
            src_ref=gram_ref.at[other],
            dst_ref=gram_ref.at[other],
            send_sem=gram_send.at[offset],
            recv_sem=gram_recv.at[other],
            device_id=(vtx, other),
            device_id_type=MESH,
        ).wait_recv()
    for copy in sent:
        copy.wait_send()


def block_diagonal(blocks):
    height, width = blocks[0].shape
    rows = []
    for index, block in enumerate(blocks):
        parts = []
        if index:
            parts.append(jnp.zeros((height, width * index), F32))
        parts.append(block)
        if index + 1 < len(blocks):
            parts.append(jnp.zeros((height, width * (len(blocks) - 1 - index)), F32))
        rows.append(jnp.concatenate(parts, axis=1) if len(parts) > 1 else parts[0])
    return jnp.concatenate(rows, axis=0) if len(rows) > 1 else rows[0]


def merge_kernel(gram_ref, product_ref, all_ref, basis_ref, coefficients_ref):
    identity_part = identity_lanes()
    width = 2 * RANK
    gram = gram_ref[...]
    merged = None
    while True:
        pairs = gram.shape[0] // width
        spaces = top_spaces(
            [gram[n * width : (n + 1) * width, n * width : (n + 1) * width] for n in range(pairs)],
            identity_part,
        )
        turn = block_diagonal(spaces)
        merged = turn if merged is None else dot(turn, merged, NN, HIGHEST)
        if pairs == 1:
            break
        gram = dot(dot(turn, gram, NN, HIGHEST), turn, NT, HIGHEST)
    merged = merged.astype(BF16)
    wide = merged.astype(F32)
    image = dot(wide, gram_ref[...], NN, HIGHEST)
    padded = jnp.concatenate([jnp.zeros_like(wide), wide], axis=0)
    factor = inverse_factors([dot(image, padded, NT, HIGHEST)], identity_part)[0]
    moments = dot(wide, product_ref[...], NN, HIGHEST)
    half_way = dot(factor, moments, NN, HIGHEST)
    coefficients_ref[...] = dot(factor, half_way, TN, HIGHEST).astype(BF16)
    basis_ref[...] = dot(merged, all_ref[...], NN).T.astype(BF16)


def project_kernel(ids_ref, mask_ref, skin_ref, basis_ref, coefficients_ref, out_ref, chosen_ref):
    slots = ids_ref.shape[1]
    blocks_here = out_ref.shape[0] // 256
    first = pl.program_id(0) * blocks_here
    for index in range(blocks_here):
        for slot in range(slots):
            place = pl.multiple_of(ids_ref[first + index, slot] * SHAPES, SHAPES)
            active = mask_ref[first + index, slot] != 0
            values = basis_ref[pl.ds(place, SHAPES), :]
            chosen_ref[index, slot * SHAPES : (slot + 1) * SHAPES, :] = jnp.where(
                active, values, jnp.zeros_like(values)
            )
        rows = skin_ref[index * 256 : (index + 1) * 256, :]
        basis = dot(rows, chosen_ref[index], NN).astype(BF16)
        out_ref[index * 256 : (index + 1) * 256, :] = dot(basis, coefficients_ref[...], NN).astype(BF16)


def params(**more):
    return pltpu.CompilerParams(vmem_limit_bytes=56 * 2**20, **more)


def per_device(skin_weights, bone_ids, slot_mask, pose_coeffs):
    rows, depth = skin_weights.shape
    bones, shapes, poses = pose_coeffs.shape
    coeffs = pose_coeffs.reshape(bones * shapes, poses)
    wide = bones * shapes
    shards = lax.axis_size("pose")
    joint = shards * RANK
    part, image = pl.pallas_call(
        leaf_kernel,
        out_shape=(
            jax.ShapeDtypeStruct((poses, poses), F32),
            jax.ShapeDtypeStruct((wide, poses), BF16),
        ),
        in_specs=[VMEM, SMEM, SMEM, VMEM],
        out_specs=(VMEM, VMEM),
        scratch_shapes=[pltpu.VMEM((depth, poses), BF16), pltpu.VMEM((wide, poses), F32)],
        compiler_params=params(),
        name="leaf",
    )(skin_weights, bone_ids, slot_mask, coeffs)
    gram = pl.pallas_call(
        gram_sum_kernel,
        out_shape=jax.ShapeDtypeStruct((poses, poses), F32),
        in_specs=[VMEM],
        out_specs=VMEM,
        scratch_shapes=sum_scratch(poses),
        compiler_params=params(collective_id=0, has_side_effects=True),
        name="gram_sum",
    )(part)
    turn, sketch = pl.pallas_call(
        turn_kernel,
        out_shape=(
            jax.ShapeDtypeStruct((RANK, poses), BF16),
            jax.ShapeDtypeStruct((RANK, wide), BF16),
        ),
        in_specs=[VMEM, VMEM],
        out_specs=(VMEM, VMEM),
        compiler_params=params(),
        name="turn",
    )(gram, coeffs)
    sketches, product, joint_gram = pl.pallas_call(
        joint_kernel,
        out_shape=(
            jax.ShapeDtypeStruct((shards, RANK, wide), BF16),
            jax.ShapeDtypeStruct((joint, poses), F32),
            jax.ShapeDtypeStruct((shards, RANK, joint), F32),
        ),
        in_specs=[VMEM, VMEM, VMEM],
        out_specs=(VMEM, VMEM, VMEM),
        scratch_shapes=[pltpu.VMEM((joint, poses), F32)]
        + sum_scratch(joint)
        + [
            pltpu.SemaphoreType.DMA((shards,)),
            pltpu.SemaphoreType.DMA((shards,)),
            pltpu.SemaphoreType.DMA((shards,)),
            pltpu.SemaphoreType.DMA((shards,)),
        ],
        compiler_params=params(collective_id=1, has_side_effects=True),
        name="joint",
    )(sketch, image, turn)
    basis, coefficients = pl.pallas_call(
        merge_kernel,
        out_shape=(
            jax.ShapeDtypeStruct((wide, RANK), BF16),
            jax.ShapeDtypeStruct((RANK, poses), BF16),
        ),
        in_specs=[VMEM, VMEM, VMEM],
        out_specs=(VMEM, VMEM),
        compiler_params=params(),
        name="merge",
    )(joint_gram.reshape(joint, joint), product, sketches.reshape(joint, wide))
    step_rows = 1024
    return pl.pallas_call(
        project_kernel,
        out_shape=jax.ShapeDtypeStruct((rows, poses), BF16),
        grid=(rows // step_rows,),
        in_specs=[
            SMEM,
            SMEM,
            pl.BlockSpec((step_rows, depth), lambda i: (i, 0)),
            VMEM,
            VMEM,
        ],
        out_specs=pl.BlockSpec((step_rows, poses), lambda i: (i, 0)),
        scratch_shapes=[pltpu.VMEM((step_rows // 256, depth, RANK), BF16)],
        compiler_params=params(),
        name="project",
    )(bone_ids, slot_mask, skin_weights, basis, coefficients)


def solution(mesh):
    in_specs = (P("vtx", None), P("vtx", None), P("vtx", None), P(None, None, "pose"))
    return jax.shard_map(
        per_device, mesh=mesh, in_specs=in_specs, out_specs=P("vtx", "pose"), check_vma=False
    )
```

time: 1250 us -> 192 us (0.15)
  the two profiles are of different devices: /device:TPU:2 before, /device:TPU:1 now
where the time goes in v1:
time: 192 us
  Pallas kernels  189 us (98%)
  local copies, waits for them, and re-layouts  2.73 us (1%)
    pallas_call x1, Pallas kernels, per_device(): pl.pallas_call(joint_kernel, out_shape=(jax.ShapeDtypeStruct((shards, RAN...  81.7 us
    pallas_call x1, Pallas kernels, per_device(): pl.pallas_call(merge_kernel, out_shape=(jax.ShapeDtypeStruct((wide, RANK)...  38 us
    pallas_call x1, Pallas kernels, per_device(): pl.pallas_call(gram_sum_kernel, out_shape=jax.ShapeDtypeStruct((poses, po...  31.5 us
    pallas_call x1, Pallas kernels, per_device(): pl.pallas_call(leaf_kernel, out_shape=(jax.ShapeDtypeStruct((poses, poses...  18 us
    pallas_call x1, Pallas kernels, per_device(): pl.pallas_call(turn_kernel, out_shape=(jax.ShapeDtypeStruct((RANK, poses)...  10.5 us
    pallas_call x1, Pallas kernels, per_device(): pl.pallas_call(project_kernel, out_shape=jax.ShapeDtypeStruct((rows, pose...  9.1 us

profile of v1, /device:TPU:1, one launch (start us, length us, event | category | flops | bytes accessed | tf_op | source)
XLA Modules:
  0.0 191.6 jit_solution(6930336856413379180)
XLA Ops:
  0.0 1.4 copy.7.ids_ref
  1.4 1.4 copy.8.mask_ref
  2.7 18.0 %leaf.1 = (f32[256,256]{1,0:T(8,128)}, bf16[4096,256]{1,0:T(8,128)(2,1)}) custom-call(bf16[8192,128]{1,0:T(8,128)(2,1)} %skin_ref.3, s32[32,4]{1,0:T(8,128)} %copy.7.ids_ref, s32[32,4]{1,0:T(8,128)} %copy.8.mask_ref, bf16[4096,256]{1,0:T(8,128)(2,1)} %bitcast.3), custom_call_target="tpu_custom_call" | custom-call | tf_op jit(solution)/shard_map/leaf/pallas_call | solution.py:422
  20.8 31.5 %gram_sum.1.gram_ref = f32[256,256]{1,0:T(8,128)} custom-call(f32[256,256]{1,0:T(8,128)} %get-tuple-element.14.part_ref), custom_call_target="tpu_custom_call" | custom-call | tf_op jit(solution)/shard_map/gram_sum/pallas_call | solution.py:434
  52.3 10.5 %turn.1 = (bf16[64,256]{1,0:T(8,128)(2,1)}, bf16[64,4096]{1,0:T(8,128)(2,1)}) custom-call(f32[256,256]{1,0:T(8,128)} %gram_sum.1.gram_ref, bf16[4096,256]{1,0:T(8,128)(2,1)} %bitcast.4), custom_call_target="tpu_custom_call" | custom-call | tf_op jit(solution)/shard_map/turn/pallas_call | solution.py:443
  62.7 81.7 %joint.1 = (bf16[8,64,4096]{2,1,0:T(8,128)(2,1)}, f32[512,256]{1,0:T(8,128)}, f32[8,64,512]{2,1,0:T(8,128)}) custom-call(bf16[64,4096]{1,0:T(8,128)(2,1)} %get-tuple-element.15.sketch_ref, bf16[4096,256]{1,0:T(8,128)(2,1)} %get-tuple-element.16.image_ref, bf16[64,256]{1,0:T(8,128)(2,1)} %get-tuple-element.17.turn_ref), custom_call_target="tpu_custom_call" | custom-call | tf_op jit(solution)/shard_map/joint/pallas_call | solution.py:454
  144.4 38.0 %merge.1 = (bf16[4096,64]{1,0:T(8,128)(2,1)}, bf16[64,256]{1,0:T(8,128)(2,1)}) custom-call(f32[512,512]{1,0:T(8,128)} %bitcast.6, f32[512,256]{1,0:T(8,128)} %get-tuple-element.19.product_ref, bf16[512,4096]{1,0:T(8,128)(2,1)} %bitcast.5), custom_call_target="tpu_custom_call" | custom-call | tf_op jit(solution)/shard_map/merge/pallas_call | solution.py:474
  182.5 9.1 %project.1 = bf16[8192,256]{1,0:T(8,128)(2,1)} custom-call(s32[32,4]{1,0:T(8,128)} %copy.7.ids_ref, s32[32,4]{1,0:T(8,128)} %copy.8.mask_ref, bf16[8192,128]{1,0:T(8,128)(2,1)} %skin_ref.3, bf16[4096,64]{1,0:T(8,128)(2,1)} %get-tuple-element.21.basis_ref, bf16[64,256]{1,0:T(8,128)(2,1)} %get-tuple-element.22.coefficients_ref), custom_call_target="tpu_custom_call" | custom-call | tf_op jit(solution)/shard_map/project/pallas_call | solution.py:486

commit v2 on v1

--- a/solution.py
+++ b/solution.py
@@ -28,32 +28,42 @@
 TN = ((0,), (0,))
 
 
-def leaf_kernel(skin_ref, ids_ref, mask_ref, coeffs_ref, gram_ref, image_ref, chosen_ref, sums_ref):
-    block_count, slots = ids_ref.shape
+def chosen_rows(ids_ref, mask_ref, source_ref, block):
+    parts = []
+    for slot in range(ids_ref.shape[0]):
+        place = pl.multiple_of(ids_ref[slot, block] * SHAPES, SHAPES)
+        values = source_ref[pl.ds(place, SHAPES), :]
+        parts.append(jnp.where(mask_ref[slot, block] != 0, values, jnp.zeros_like(values)))
+    return jnp.concatenate(parts, axis=0)
+
+
+def leaf_kernel(skin_ref, ids_ref, mask_ref, coeffs_ref, gram_ref, image_ref, slab_ref, sums_ref):
+    slots, block_count = ids_ref.shape
     block_rows = skin_ref.shape[0] // block_count
+    group = slab_ref.shape[0] // block_rows
     sums_ref[...] = jnp.zeros_like(sums_ref)
     gram_ref[...] = jnp.zeros_like(gram_ref)
 
-    def step(block, carry):
-        for slot in range(slots):
-            place = pl.multiple_of(ids_ref[block, slot] * SHAPES, SHAPES)
-            values = coeffs_ref[pl.ds(place, SHAPES), :]
-            active = mask_ref[block, slot] != 0
-            chosen_ref[slot * SHAPES : (slot + 1) * SHAPES, :] = jnp.where(
-                active, values, jnp.zeros_like(values)
-            )
-        rows = skin_ref[pl.ds(pl.multiple_of(block * block_rows, block_rows), block_rows), :]
-        slab = dot(rows, chosen_ref[...], NN).astype(BF16)
-        gram_ref[...] += dot(slab, slab, TN)
-        image = dot(rows, slab, TN)
-        for slot in range(slots):
-            place = pl.multiple_of(ids_ref[block, slot] * SHAPES, SHAPES)
-            active = mask_ref[block, slot] != 0
-            values = image[slot * SHAPES : (slot + 1) * SHAPES, :]
-            sums_ref[pl.ds(place, SHAPES), :] += jnp.where(active, values, jnp.zeros_like(values))
+    def step(index, carry):
+        images = []
+        for inside in range(group):
+            block = index * group + inside
+            rows = skin_ref[pl.ds(pl.multiple_of(block * block_rows, block_rows), block_rows), :]
+            slab = dot(rows, chosen_rows(ids_ref, mask_ref, coeffs_ref, block), NN).astype(BF16)
+            slab_ref[inside * block_rows : (inside + 1) * block_rows, :] = slab
+            images.append(dot(rows, slab, TN))
+        gram_ref[...] += dot(slab_ref[...], slab_ref[...], TN)
+        for inside in range(group):
+            block = index * group + inside
+            for slot in range(slots):
+                place = pl.multiple_of(ids_ref[slot, block] * SHAPES, SHAPES)
+                values = images[inside][slot * SHAPES : (slot + 1) * SHAPES, :]
+                sums_ref[pl.ds(place, SHAPES), :] += jnp.where(
+                    mask_ref[slot, block] != 0, values, jnp.zeros_like(values)
+                )
         return carry
 
-    lax.fori_loop(0, block_count, step, 0)
+    lax.fori_loop(0, block_count // group, step, 0)
     image_ref[...] = sums_ref[...].astype(BF16)
 
 
@@ -194,20 +204,22 @@
     from_chunks(total, gram_ref)
 
 
-def sum_scratch(rows):
-    return [pltpu.VMEM((2, SIDE, rows // SIDE, 128), F32)] * 4 + [
-        pltpu.SemaphoreType.DMA((2, SIDE))
+def sum_scratch(rows, groups=()):
+    return [pltpu.VMEM((*groups, 2, SIDE, rows // SIDE, 128), F32)] * 4 + [
+        pltpu.SemaphoreType.DMA((*groups, 2, SIDE))
     ] * 6
 
 
-def inverse_factors(grams, identity_part):
+def inverse_factors(grams):
     count = len(grams)
     groups = RANK // 8
-    rows = [[gram[8 * g : 8 * g + 8] for g in range(groups)] for gram in grams]
     sublane = lax.broadcasted_iota(jnp.int32, (8, 128), 0)
-    for n in range(count):
-        for g in range(groups):
-            rows[n][g] = rows[n][g] + identity_part[8 * g : 8 * g + 8]
+    lane = lax.broadcasted_iota(jnp.int32, (8, 128), 1)
+    rows = [
+        [gram[8 * g : 8 * g + 8] + jnp.where(lane == sublane + 8 * g, 1.0, 0.0) for g in range(groups)]
+        for gram in grams
+    ]
+    squares = []
     for p in range(groups):
         for n in range(count):
             own = rows[n]
@@ -236,116 +248,238 @@
                     for d in range(c + 1, 8):
                         spread[d][g - p] = spread[d][g - p] - column * leads[d - c - 1]
             own[p] = own[p] * lax.rsqrt(pivots)
-    return [jnp.concatenate(own, axis=0)[:, :RANK] for own in rows]
-
-
-def identity_lanes():
-    row = lax.broadcasted_iota(jnp.int32, (RANK, 128), 0)
-    lane = lax.broadcasted_iota(jnp.int32, (RANK, 128), 1)
-    return jnp.where(row == lane, 1.0, 0.0).astype(F32)
-
-
-def orthonormal(columns, identity_part):
+            squares.append((n, pivots))
+    factors = [jnp.concatenate(own, axis=0)[:, :RANK] for own in rows]
+    return factors, [[value for m, value in squares if m == n] for n in range(count)]
+
+
+def factors_of(columns):
     grams = []
     for value in columns:
         padded = jnp.concatenate([jnp.zeros_like(value), value], axis=0)
         grams.append(dot(value, padded, NT, HIGHEST))
-    factors = inverse_factors(grams, identity_part)
-    return [dot(factor, value, NN, HIGHEST) for factor, value in zip(factors, columns)]
-
-
-def top_spaces(grams, identity_part):
-    columns = orthonormal([gram[:RANK, :] for gram in grams], identity_part)
+    return inverse_factors(grams)
+
+
+def top_spaces(grams, out_ref):
+    columns = []
+    scaled = []
+    for gram in grams:
+        size = gram.shape[0]
+        diagonal = lax.broadcasted_iota(jnp.int32, (size, size), 0) == lax.broadcasted_iota(
+            jnp.int32, (size, size), 1
+        )
+        largest = jnp.max(
+            jnp.max(jnp.where(diagonal, gram, 0.0), axis=0, keepdims=True), axis=1, keepdims=True
+        )
+        scaled.append(gram * (1.0 / largest))
+        columns.append(scaled[-1][:RANK, :])
     for sweep in range(SWEEPS - 1):
-        columns = orthonormal(
-            [dot(value, gram, NN, HIGHEST) for value, gram in zip(columns, grams)], identity_part
-        )
-    return columns
-
-
-def turn_kernel(gram_ref, coeffs_ref, turn_ref, sketch_ref):
-    turn = top_spaces([gram_ref[...]], identity_lanes())[0].astype(BF16)
+        columns = [dot(value, gram, NN, HIGHEST) for value, gram in zip(columns, scaled)]
+    factors, squares = factors_of(columns)
+    worst = None
+    for n, (factor, value) in enumerate(zip(factors, columns)):
+        out_ref[n] = dot(factor, value, NN, HIGHEST)
+        low = functools.reduce(jnp.minimum, squares[n])
+        high = functools.reduce(jnp.maximum, squares[n])
+        ratio = jnp.min(low) / jnp.max(high)
+        good = ratio > 2e-5
+        worst = good if worst is None else jnp.logical_and(worst, good)
+
+    @pl.when(jnp.logical_not(worst))
+    def _():
+        row = lax.broadcasted_iota(jnp.int32, grams[0].shape, 0)
+        lane = lax.broadcasted_iota(jnp.int32, grams[0].shape, 1)
+        for n in range(len(grams)):
+            out_ref[n] = jnp.where(row == lane, 1.0, 0.0).astype(F32)[:RANK]
+
+        def sweep(index, carry):
+            values = [dot(out_ref[n], gram, NN, HIGHEST) for n, gram in enumerate(grams)]
+            for n, (factor, value) in enumerate(zip(factors_of(values)[0], values)):
+                out_ref[n] = dot(factor, value, NN, HIGHEST)
+            return carry
+
+        lax.fori_loop(0, SWEEPS, sweep, 0)
+
+    return [out_ref[n] for n in range(len(grams))]
+
+
+def turn_kernel(gram_ref, coeffs_ref, turn_ref, sketch_ref, space_ref):
+    turn = top_spaces([gram_ref[...]], space_ref)[0].astype(BF16)
     turn_ref[...] = turn
     sketch_ref[...] = dot(turn, coeffs_ref[...], NT).astype(BF16)
 
 
 def joint_kernel(sketch_ref, image_ref, turn_ref, all_ref, product_ref, gram_ref, *scratch):
-    partial_ref, source, first, second, total = scratch[:5]
-    sems = scratch[5:11]
-    send_sem, recv_sem, gram_send, gram_recv = scratch[11:]
+    source, first, second, total = scratch[:4]
+    sems = scratch[4:10]
+    send_sem, recv_sem, gram_send, gram_recv = scratch[10:]
     place = my_place()
     z, y, pose = place
     vtx = z * SIDE + y
     poses = all_ref.shape[0]
     chips = poses // 2
+    width = 2 * RANK
+    middle = RANK // 2
     x, core = pose // 2, lax.rem(pose, 2)
     sibling = (vtx, x * 2 + 1 - core)
-    pose_devices = [(vtx, lax.rem(pose + offset, poses)) for offset in range(1, poses)]
-    greet(vtx_devices(*place) + pose_devices)
-
-    def send(source_ref, slot, device, number):
+    chip_at = [lax.rem(x + group, chips) for group in range(chips)]
+    peer = [(vtx, chip * 2 + core) for chip in chip_at]
+    outer, inner = ("y", "z"), ("z", "y")
+    mine = {"y": y, "z": z}
+    greet(vtx_devices(*place) + [(vtx, lax.rem(pose + offset, poses)) for offset in range(1, poses)])
+    sent = []
+
+    def send(source_ref, target_ref, arrival, device, number):
         copy = pltpu.make_async_remote_copy(
             src_ref=source_ref,
-            dst_ref=all_ref.at[slot],
+            dst_ref=target_ref,
             send_sem=send_sem.at[number],
-            recv_sem=recv_sem.at[slot],
+            recv_sem=arrival,
             device_id=device,
             device_id_type=MESH,
         )
         copy.start()
-        return copy
-
-    def wait_for(slot, device):
+        sent.append(copy)
+
+    def wait_for(target_ref, arrival, device):
         pltpu.make_async_remote_copy(
-            src_ref=all_ref.at[slot],
-            dst_ref=all_ref.at[slot],
+            src_ref=target_ref,
+            dst_ref=target_ref,
             send_sem=send_sem.at[0],
-            recv_sem=recv_sem.at[slot],
+            recv_sem=arrival,
             device_id=device,
             device_id_type=MESH,
         ).wait_recv()
 
-    sent = []
-    for offset in (1, chips - 1, 2):
-        other = lax.rem(x + offset, chips)
-        sent.append(send(sketch_ref, pose, (vtx, other * 2 + core), offset))
-    sent.append(send(sketch_ref, pose, sibling, 0))
-    all_ref[pose] = sketch_ref[...]
-    for offset in (1, chips - 1, 2):
-        other = lax.rem(x + offset, chips)
-        slot = other * 2 + core
-        wait_for(slot, (vtx, slot))
-        sent.append(send(all_ref.at[slot], slot, sibling, chips + offset))
-    for offset in range(chips):
-        slot = lax.rem(x + offset, chips) * 2 + 1 - core
-        wait_for(slot, sibling)
-    for index in range(poses):
-        partial_ref[index * RANK : (index + 1) * RANK, :] = dot(all_ref[index], image_ref[...], NN)
-    to_chunks(partial_ref, source)
-    vtx_sum(source, first, second, total, sems, place)
-    from_chunks(total, product_ref)
-    gram_ref[pose] = dot(turn_ref[...].astype(F32), product_ref[...], NT, HIGHEST)
-    for offset in range(1, poses):
-        copy = pltpu.make_async_remote_copy(
-            src_ref=gram_ref.at[pose],
-            dst_ref=gram_ref.at[pose],
-            send_sem=gram_send.at[offset],
-            recv_sem=gram_recv.at[pose],
-            device_id=(vtx, lax.rem(pose + offset, poses)),
-            device_id_type=MESH,
+    def half_of(slot, half):
+        return all_ref.at[slot, pl.ds(half * middle, middle)]
+
+    def start_sum(group):
+        for index in range(2):
+            part = dot(all_ref[chip_at[group] * 2 + index], image_ref[...], NN)
+            depth = width // SIDE
+            for chunk in range(SIDE // 2):
+                for half in range(2):
+                    source[group, half, index * (SIDE // 2) + chunk] = part[
+                        chunk * depth : (chunk + 1) * depth, half * 128 : (half + 1) * 128
+                    ]
+        sent.extend(
+            exchange(
+                2,
+                outer,
+                lambda h, o: source.at[group, h, o],
+                lambda h, m: first.at[group, h, m],
+                sems[0].at[group],
+                sems[1].at[group],
+                place,
+            )
         )
-        copy.start()
-        sent.append(copy)
-    for offset in range(1, poses):
-        other = lax.rem(pose + offset, poses)
-        pltpu.make_async_remote_copy(
-            src_ref=gram_ref.at[other],
-            dst_ref=gram_ref.at[other],
-            send_sem=gram_send.at[offset],
-            recv_sem=gram_recv.at[other],
-            device_id=(vtx, other),
-            device_id_type=MESH,
-        ).wait_recv()
+
+    def second_leg(group):
+        for half in range(2):
+            arrived(
+                half, outer[half], lambda h, o: first.at[group, h, o], sems[0].at[group], sems[1].at[group], place
+            )
+            me = mine[outer[half]]
+            first[group, half, me] = source[group, half, me]
+            value = first[group, half, 0]
+            for index in range(1, SIDE):
+                value += first[group, half, index]
+            second[group, half, mine[inner[half]]] = value
+            sent.extend(
+                exchange_one(half, inner[half], second.at[group], sems[2].at[group], sems[3].at[group], place)
+            )
+
+    def third_leg(group):
+        for half in range(2):
+            arrived(
+                half, inner[half], lambda h, o: second.at[group, h, o], sems[2].at[group], sems[3].at[group], place
+            )
+            value = second[group, half, 0]
+            for index in range(1, SIDE):
+                value += second[group, half, index]
+            total[group, half, mine[outer[half]]] = value
+            sent.extend(
+                exchange_one(half, outer[half], total.at[group], sems[4].at[group], sems[5].at[group], place)
+            )
+
+    def end_sum(group):
+        for half in range(2):
+            arrived(
+                half, outer[half], lambda h, o: total.at[group, h, o], sems[4].at[group], sems[5].at[group], place
+            )
+        row = pl.multiple_of(chip_at[group] * width, width)
+        for half in range(2):
+            product_ref[pl.ds(row, width), half * 128 : (half + 1) * 128] = total[group, half].reshape(width, 128)
+
+    def gram_part(group):
+        row = pl.multiple_of(chip_at[group] * width, width)
+        gram_ref[chip_at[group], pose] = dot(
+            turn_ref[...].astype(F32), product_ref[pl.ds(row, width), :], NT, HIGHEST
+        )
+        for offset in range(1, poses):
+            copy = pltpu.make_async_remote_copy(
+                src_ref=gram_ref.at[chip_at[group], pose],
+                dst_ref=gram_ref.at[chip_at[group], pose],
+                send_sem=gram_send.at[group, offset],
+                recv_sem=gram_recv.at[group, pose],
+                device_id=(vtx, lax.rem(pose + offset, poses)),
+                device_id_type=MESH,
+            )
+            copy.start()
+            sent.append(copy)
+
+    def gram_arrived(group):
+        for offset in range(1, poses):
+            other = lax.rem(pose + offset, poses)
+            chip = lax.rem(other // 2 + group, chips)
+            wait_for(gram_ref.at[chip, other], gram_recv.at[group, other], (vtx, other))
+
+    own = pose
+    up, down, across = [chip_at[g] * 2 + core for g in (1, 3, 2)]
+    send(sketch_ref, all_ref.at[own], recv_sem.at[0, own], peer[1], 0)
+    send(sketch_ref, all_ref.at[own], recv_sem.at[0, own], peer[3], 1)
+    send(sketch_ref, all_ref.at[own], recv_sem.at[0, own], sibling, 2)
+    all_ref[own] = sketch_ref[...]
+    other = sibling[1]
+    wait_for(all_ref.at[other], recv_sem.at[0, other], sibling)
+    start_sum(0)
+    second_leg(0)
+    wait_for(all_ref.at[down], recv_sem.at[0, down], peer[3])
+    send(half_of(down, 0), half_of(down, 0), recv_sem.at[0, down], peer[1], 3)
+    send(all_ref.at[down], all_ref.at[down], recv_sem.at[0, down], sibling, 4)
+    wait_for(all_ref.at[up], recv_sem.at[0, up], peer[1])
+    send(half_of(up, 1), half_of(up, 1), recv_sem.at[1, up], peer[3], 5)
+    send(all_ref.at[up], all_ref.at[up], recv_sem.at[0, up], sibling, 6)
+    third_leg(0)
+    for group in (3, 1):
+        slot = chip_at[group] * 2 + 1 - core
+        wait_for(all_ref.at[slot], recv_sem.at[0, slot], sibling)
+        start_sum(group)
+    end_sum(0)
+    gram_part(0)
+    second_leg(3)
+    second_leg(1)
+    wait_for(half_of(across, 0), recv_sem.at[0, across], peer[3])
+    send(half_of(across, 0), half_of(across, 0), recv_sem.at[0, across], sibling, 7)
+    wait_for(half_of(across, 1), recv_sem.at[1, across], peer[1])
+    send(half_of(across, 1), half_of(across, 1), recv_sem.at[1, across], sibling, 8)
+    slot = chip_at[2] * 2 + 1 - core
+    wait_for(half_of(slot, 0), recv_sem.at[0, slot], sibling)
+    wait_for(half_of(slot, 1), recv_sem.at[1, slot], sibling)
+    start_sum(2)
+    third_leg(3)
+    third_leg(1)
+    second_leg(2)
+    end_sum(1)
+    gram_part(1)
+    third_leg(2)
+    end_sum(3)
+    end_sum(2)
+    gram_part(2)
+    for group in (0, 1, 2):
+        gram_arrived(group)
     for copy in sent:
         copy.wait_send()
 
@@ -364,16 +498,31 @@
     return jnp.concatenate(rows, axis=0) if len(rows) > 1 else rows[0]
 
 
-def merge_kernel(gram_ref, product_ref, all_ref, basis_ref, coefficients_ref):
-    identity_part = identity_lanes()
+def merge_kernel(rows_ref, product_ref, all_ref, basis_ref, coefficients_ref, joint_ref, space_ref):
     width = 2 * RANK
-    gram = gram_ref[...]
+    chips = rows_ref.shape[0]
+    for chip in range(chips):
+        for other in range(chips):
+            behind = (chip - other) % chips == 1
+            for index in range(2):
+                if behind:
+                    continue
+                joint_ref[
+                    chip * width + index * RANK : chip * width + (index + 1) * RANK,
+                    other * width : (other + 1) * width,
+                ] = rows_ref[other, 2 * chip + index]
+    for chip in range(chips):
+        other = (chip - 1) % chips
+        joint_ref[chip * width : (chip + 1) * width, other * width : (other + 1) * width] = joint_ref[
+            other * width : (other + 1) * width, chip * width : (chip + 1) * width
+        ].T
+    gram = joint_ref[...]
     merged = None
     while True:
         pairs = gram.shape[0] // width
         spaces = top_spaces(
             [gram[n * width : (n + 1) * width, n * width : (n + 1) * width] for n in range(pairs)],
-            identity_part,
+            space_ref,
         )
         turn = block_diagonal(spaces)
         merged = turn if merged is None else dot(turn, merged, NN, HIGHEST)
@@ -382,34 +531,29 @@
         gram = dot(dot(turn, gram, NN, HIGHEST), turn, NT, HIGHEST)
     merged = merged.astype(BF16)
     wide = merged.astype(F32)
-    image = dot(wide, gram_ref[...], NN, HIGHEST)
+    image = dot(wide, joint_ref[...], NN, HIGHEST)
     padded = jnp.concatenate([jnp.zeros_like(wide), wide], axis=0)
-    factor = inverse_factors([dot(image, padded, NT, HIGHEST)], identity_part)[0]
+    factor = inverse_factors([dot(image, padded, NT, HIGHEST)])[0][0]
     moments = dot(wide, product_ref[...], NN, HIGHEST)
     half_way = dot(factor, moments, NN, HIGHEST)
     coefficients_ref[...] = dot(factor, half_way, TN, HIGHEST).astype(BF16)
     basis_ref[...] = dot(merged, all_ref[...], NN).T.astype(BF16)
 
 
-def project_kernel(ids_ref, mask_ref, skin_ref, basis_ref, coefficients_ref, out_ref, chosen_ref):
-    slots = ids_ref.shape[1]
-    blocks_here = out_ref.shape[0] // 256
+def project_kernel(ids_ref, mask_ref, skin_ref, basis_ref, coefficients_ref, out_ref, rows_ref):
+    block_count = ids_ref.shape[1]
+    blocks_here = block_count // pl.num_programs(0)
+    block_rows = out_ref.shape[0] // blocks_here
     first = pl.program_id(0) * blocks_here
     for index in range(blocks_here):
-        for slot in range(slots):
-            place = pl.multiple_of(ids_ref[first + index, slot] * SHAPES, SHAPES)
-            active = mask_ref[first + index, slot] != 0
-            values = basis_ref[pl.ds(place, SHAPES), :]
-            chosen_ref[index, slot * SHAPES : (slot + 1) * SHAPES, :] = jnp.where(
-                active, values, jnp.zeros_like(values)
-            )
-        rows = skin_ref[index * 256 : (index + 1) * 256, :]
-        basis = dot(rows, chosen_ref[index], NN).astype(BF16)
-        out_ref[index * 256 : (index + 1) * 256, :] = dot(basis, coefficients_ref[...], NN).astype(BF16)
-
-
-def params(**more):
-    return pltpu.CompilerParams(vmem_limit_bytes=56 * 2**20, **more)
+        chosen = chosen_rows(ids_ref, mask_ref, basis_ref, first + index)
+        here = slice(index * block_rows, (index + 1) * block_rows)
+        rows_ref[here, :] = dot(skin_ref[here, :], chosen, NN).astype(BF16)
+    out_ref[...] = dot(rows_ref[...], coefficients_ref[...], NN).astype(BF16)
+
+
+def params(mebibytes, **more):
+    return pltpu.CompilerParams(vmem_limit_bytes=mebibytes * 2**20, **more)
 
 
 def per_device(skin_weights, bone_ids, slot_mask, pose_coeffs):
@@ -419,6 +563,7 @@
     wide = bones * shapes
     shards = lax.axis_size("pose")
     joint = shards * RANK
+    bone_ids, slot_mask = bone_ids.T, slot_mask.T
     part, image = pl.pallas_call(
         leaf_kernel,
         out_shape=(
@@ -427,8 +572,8 @@
         ),
         in_specs=[VMEM, SMEM, SMEM, VMEM],
         out_specs=(VMEM, VMEM),
-        scratch_shapes=[pltpu.VMEM((depth, poses), BF16), pltpu.VMEM((wide, poses), F32)],
-        compiler_params=params(),
+        scratch_shapes=[pltpu.VMEM((rows // 4, poses), BF16), pltpu.VMEM((wide, poses), F32)],
+        compiler_params=params(24),
         name="leaf",
     )(skin_weights, bone_ids, slot_mask, coeffs)
     gram = pl.pallas_call(
@@ -437,7 +582,7 @@
         in_specs=[VMEM],
         out_specs=VMEM,
         scratch_shapes=sum_scratch(poses),
-        compiler_params=params(collective_id=0, has_side_effects=True),
+        compiler_params=params(8, collective_id=0, has_side_effects=True),
         name="gram_sum",
     )(part)
     turn, sketch = pl.pallas_call(
@@ -448,7 +593,8 @@
         ),
         in_specs=[VMEM, VMEM],
         out_specs=(VMEM, VMEM),
-        compiler_params=params(),
+        scratch_shapes=[pltpu.VMEM((1, RANK, poses), F32)],
+        compiler_params=params(12),
         name="turn",
     )(gram, coeffs)
     sketches, product, joint_gram = pl.pallas_call(
@@ -456,19 +602,18 @@
         out_shape=(
             jax.ShapeDtypeStruct((shards, RANK, wide), BF16),
             jax.ShapeDtypeStruct((joint, poses), F32),
-            jax.ShapeDtypeStruct((shards, RANK, joint), F32),
+            jax.ShapeDtypeStruct((shards // 2, shards, RANK, 2 * RANK), F32),
         ),
         in_specs=[VMEM, VMEM, VMEM],
         out_specs=(VMEM, VMEM, VMEM),
-        scratch_shapes=[pltpu.VMEM((joint, poses), F32)]
-        + sum_scratch(joint)
+        scratch_shapes=sum_scratch(2 * RANK, (shards // 2,))
         + [
-            pltpu.SemaphoreType.DMA((shards,)),
-            pltpu.SemaphoreType.DMA((shards,)),
-            pltpu.SemaphoreType.DMA((shards,)),
-            pltpu.SemaphoreType.DMA((shards,)),
+            pltpu.SemaphoreType.DMA((9,)),
+            pltpu.SemaphoreType.DMA((2, shards)),
+            pltpu.SemaphoreType.DMA((3, shards)),
+            pltpu.SemaphoreType.DMA((3, shards)),
         ],
-        compiler_params=params(collective_id=1, has_side_effects=True),
+        compiler_params=params(20, collective_id=1, has_side_effects=True),
         name="joint",
     )(sketch, image, turn)
     basis, coefficients = pl.pallas_call(
@@ -479,10 +624,14 @@
         ),
         in_specs=[VMEM, VMEM, VMEM],
         out_specs=(VMEM, VMEM),
-        compiler_params=params(),
+        scratch_shapes=[
+            pltpu.VMEM((joint, joint), F32),
+            pltpu.VMEM((shards // 2, RANK, 2 * RANK), F32),
+        ],
+        compiler_params=params(24),
         name="merge",
-    )(joint_gram.reshape(joint, joint), product, sketches.reshape(joint, wide))
-    step_rows = 1024
+    )(joint_gram, product, sketches.reshape(joint, wide))
+    step_rows = rows // 2
     return pl.pallas_call(
         project_kernel,
         out_shape=jax.ShapeDtypeStruct((rows, poses), BF16),
@@ -495,8 +644,8 @@
             VMEM,
         ],
         out_specs=pl.BlockSpec((step_rows, poses), lambda i: (i, 0)),
-        scratch_shapes=[pltpu.VMEM((step_rows // 256, depth, RANK), BF16)],
-        compiler_params=params(),
+        scratch_shapes=[pltpu.VMEM((step_rows, RANK), BF16)],
+        compiler_params=params(24),
         name="project",
     )(bone_ids, slot_mask, skin_weights, basis, coefficients)
 

time: 192 us -> 125 us (0.65)
  Pallas kernels: 189 us -> 121 us
    pallas_call x1, Pallas kernels: 81.7 us -> 56.7 us  [per_device(): pl.pallas_call(joint_kernel, out_shape=(jax.ShapeDtypeStruct((shards, RAN...]
    pallas_call x1, Pallas kernels: 38 us -> 17.4 us  [per_device(): pl.pallas_call(merge_kernel, out_shape=(jax.ShapeDtypeStruct((wide, RANK)...]
    pallas_call x1, Pallas kernels: 18 us -> 8.77 us  [per_device(): pl.pallas_call(leaf_kernel, out_shape=(jax.ShapeDtypeStruct((poses, poses...]
    pallas_call x1, Pallas kernels: 10.5 us -> 3.85 us  [per_device(): pl.pallas_call(turn_kernel, out_shape=(jax.ShapeDtypeStruct((RANK, poses)...]
    pallas_call x1, Pallas kernels: 9.1 us -> 3.97 us  [per_device(): pl.pallas_call(project_kernel, out_shape=jax.ShapeDtypeStruct((rows, pose...]
    unnamed x2 -> x10, local copies, waits for them, and re-layouts: 2.73 us -> 4.55 us
where the time goes in v2:
time: 125 us
  Pallas kernels  121 us (97%)
  local copies, waits for them, and re-layouts  4.55 us (4%)
    pallas_call x1, Pallas kernels, per_device(): pl.pallas_call(joint_kernel, out_shape=(jax.ShapeDtypeStruct((shards, RAN...  56.7 us
    pallas_call x1, Pallas kernels, per_device(): pl.pallas_call(gram_sum_kernel, out_shape=jax.ShapeDtypeStruct((poses, po...  29.9 us
    pallas_call x1, Pallas kernels, per_device(): pl.pallas_call(merge_kernel, out_shape=(jax.ShapeDtypeStruct((wide, RANK)...  17.4 us
    pallas_call x1, Pallas kernels, per_device(): pl.pallas_call(leaf_kernel, out_shape=(jax.ShapeDtypeStruct((poses, poses...  8.77 us
    unnamed x10, local copies, waits for them, and re-layouts  4.55 us
    pallas_call x1, Pallas kernels, per_device(): pl.pallas_call(project_kernel, out_shape=jax.ShapeDtypeStruct((rows, pose...  3.97 us
    pallas_call x1, Pallas kernels, per_device(): pl.pallas_call(turn_kernel, out_shape=(jax.ShapeDtypeStruct((RANK, poses)...  3.85 us

profile of v2, /device:TPU:1, one launch (start us, length us, event | category | flops | bytes accessed | tf_op | source)
XLA Modules:
  0.0 125.2 jit_solution(15462439467138919798)
XLA Ops:
  0.0 0.0 copy-start
  0.0 1.6 %copy-done = bf16[8192,128]{1,0:T(8,128)(2,1)S(1)} copy-done((bf16[8192,128]{1,0:T(8,128)(2,1)S(1)}, bf16[8192,128]{1,0:T(8,128)(2,1)}, u32[]{:S(2)}) %copy-start) | copy-done | bytes 2097176
  1.6 0.0 copy-start.2
  1.6 1.6 %copy-done.2 = bf16[128,32,256]{2,1,0:T(8,128)(2,1)S(1)} copy-done((bf16[128,32,256]{2,1,0:T(8,128)(2,1)S(1)}, bf16[128,32,256]{2,1,0:T(8,128)(2,1)}, u32[]{:S(2)}) %copy-start.2) | copy-done | bytes 2097176
  3.2 0.0 copy-start.3
  3.2 0.7 copy-done.3
  3.9 0.0 copy-start.4
  3.9 0.7 copy-done.4
  4.5 8.8 %leaf.1 = (f32[256,256]{1,0:T(8,128)S(1)}, bf16[4096,256]{1,0:T(8,128)(2,1)S(1)}) custom-call(bf16[8192,128]{1,0:T(8,128)(2,1)S(1)} %copy-done, s32[4,32]{1,0:T(4,128)S(1)} %bitcast.7, s32[4,32]{1,0:T(4,128)S(1)} %bitcast.9, bf16[4096,256]{1,0:T(8,128)(2,1)S(1)} %bitcast.4), custom_call_target="tpu_custom_call" | custom-call | tf_op jit(solution)/shard_map/leaf/pallas_call | solution.py:567
  13.3 29.9 %gram_sum.1.gram_ref = f32[256,256]{1,0:T(8,128)S(1)} custom-call(f32[256,256]{1,0:T(8,128)S(1)} %get-tuple-element.14.part_ref), custom_call_target="tpu_custom_call" | custom-call | tf_op jit(solution)/shard_map/gram_sum/pallas_call | solution.py:579
  43.3 3.9 %turn.1 = (bf16[64,256]{1,0:T(8,128)(2,1)S(1)}, bf16[64,4096]{1,0:T(8,128)(2,1)S(1)}) custom-call(f32[256,256]{1,0:T(8,128)S(1)} %gram_sum.1.gram_ref, bf16[4096,256]{1,0:T(8,128)(2,1)S(1)} %bitcast.5), custom_call_target="tpu_custom_call" | custom-call | tf_op jit(solution)/shard_map/turn/pallas_call | solution.py:588
  47.1 56.7 %joint.1 = (bf16[8,64,4096]{2,1,0:T(8,128)(2,1)S(1)}, f32[512,256]{1,0:T(8,128)S(1)}, f32[4,8,64,128]{3,2,1,0:T(8,128)S(1)}) custom-call(bf16[64,4096]{1,0:T(8,128)(2,1)S(1)} %get-tuple-element.15.sketch_ref, bf16[4096,256]{1,0:T(8,128)(2,1)S(1)} %get-tuple-element.16.image_ref, bf16[64,256]{1,0:T(8,128)(2,1)S(1)} %get-tuple-element.17.turn_ref), custom_call_target="tpu_custom_call" | custom-call | tf_op jit(solution)/shard_map/joint/pallas_call | solution.py:600
  103.8 0.0 copy-start.1
  103.9 17.4 %merge.1 = (bf16[4096,64]{1,0:T(8,128)(2,1)S(1)}, bf16[64,256]{1,0:T(8,128)(2,1)S(1)}) custom-call(f32[4,8,64,128]{3,2,1,0:T(8,128)S(1)} %get-tuple-element.18.rows_ref, f32[512,256]{1,0:T(8,128)S(1)} %get-tuple-element.19.product_ref, bf16[512,4096]{1,0:T(8,128)(2,1)S(1)} %bitcast.6), custom_call_target="tpu_custom_call" | custom-call | tf_op jit(solution)/shard_map/merge/pallas_call | solution.py:619
  121.3 0.0 copy-done.1
  121.3 4.0 %project.1 = bf16[8192,256]{1,0:T(8,128)(2,1)} custom-call(s32[4,32]{1,0:T(4,128)S(1)} %bitcast.8, s32[4,32]{1,0:T(4,128)S(1)} %bitcast.10, bf16[8192,128]{1,0:T(8,128)(2,1)S(1)} %copy-done.1, bf16[4096,64]{1,0:T(8,128)(2,1)S(1)} %get-tuple-element.21.basis_ref, bf16[64,256]{1,0:T(8,128)(2,1)S(1)} %get-tuple-element.22.coefficients_ref), custom_call_target="tpu_custom_call" | custom-call | tf_op jit(solution)/shard_map/project/pallas_call | solution.py:635
Async XLA Ops:
  0.0 1.6 %copy-start = (bf16[8192,128]{1,0:T(8,128)(2,1)S(1)}, bf16[8192,128]{1,0:T(8,128)(2,1)}, u32[]{:S(2)}) copy-start(bf16[8192,128]{1,0:T(8,128)(2,1)} %skin_ref.3) | copy-start | bytes 6291460
  1.6 1.6 %copy-start.2 = (bf16[128,32,256]{2,1,0:T(8,128)(2,1)S(1)}, bf16[128,32,256]{2,1,0:T(8,128)(2,1)}, u32[]{:S(2)}) copy-start(bf16[128,32,256]{2,1,0:T(8,128)(2,1)} %param.7) | copy-start | bytes 6291460
  3.2 0.7 copy-start.3
  3.9 0.7 copy-start.4
  103.8 17.4 %copy-start.1 = (bf16[8192,128]{1,0:T(8,128)(2,1)S(1)}, bf16[8192,128]{1,0:T(8,128)(2,1)}, u32[]{:S(2)}) copy-start(bf16[8192,128]{1,0:T(8,128)(2,1)} %skin_ref.3) | copy-start | bytes 6291460

commit v3 on v2

--- a/solution.py
+++ b/solution.py
@@ -80,10 +80,12 @@
     return other, (other * SIDE + y, pose)
 
 
-def greet(devices):
+def greet(devices, meanwhile=None):
     barrier = pltpu.get_barrier_semaphore()
     for device in devices:
         pl.semaphore_signal(barrier, inc=1, device_id=device, device_id_type=MESH)
+    if meanwhile is not None:
+        meanwhile()
     pl.semaphore_wait(barrier, len(devices))
 
 
@@ -198,8 +200,7 @@
 
 def gram_sum_kernel(part_ref, gram_ref, source, first, second, total, *sems):
     place = my_place()
-    to_chunks(part_ref, source)
-    greet(vtx_devices(*place))
+    greet(vtx_devices(*place), lambda: to_chunks(part_ref, source))
     vtx_sum(source, first, second, total, sems, place)
     from_chunks(total, gram_ref)
 
@@ -304,13 +305,11 @@
     return [out_ref[n] for n in range(len(grams))]
 
 
-def turn_kernel(gram_ref, coeffs_ref, turn_ref, sketch_ref, space_ref):
-    turn = top_spaces([gram_ref[...]], space_ref)[0].astype(BF16)
-    turn_ref[...] = turn
-    sketch_ref[...] = dot(turn, coeffs_ref[...], NT).astype(BF16)
-
-
-def joint_kernel(sketch_ref, image_ref, turn_ref, all_ref, product_ref, gram_ref, *scratch):
+def turn_kernel(gram_ref, turn_ref, space_ref):
+    turn_ref[...] = top_spaces([gram_ref[...]], space_ref)[0].astype(BF16)
+
+
+def joint_kernel(coeffs_ref, image_ref, turn_ref, all_ref, product_ref, gram_ref, *scratch):
     source, first, second, total = scratch[:4]
     sems = scratch[4:10]
     send_sem, recv_sem, gram_send, gram_recv = scratch[10:]
@@ -327,7 +326,14 @@
     peer = [(vtx, chip * 2 + core) for chip in chip_at]
     outer, inner = ("y", "z"), ("z", "y")
     mine = {"y": y, "z": z}
-    greet(vtx_devices(*place) + [(vtx, lax.rem(pose + offset, poses)) for offset in range(1, poses)])
+
+    def own_sketch():
+        all_ref[pose] = dot(turn_ref[...], coeffs_ref[...], NT).astype(BF16)
+
+    greet(
+        vtx_devices(*place) + [(vtx, lax.rem(pose + offset, poses)) for offset in range(1, poses)],
+        own_sketch,
+    )
     sent = []
 
     def send(source_ref, target_ref, arrival, device, number):
@@ -356,14 +362,14 @@
         return all_ref.at[slot, pl.ds(half * middle, middle)]
 
     def start_sum(group):
-        for index in range(2):
-            part = dot(all_ref[chip_at[group] * 2 + index], image_ref[...], NN)
-            depth = width // SIDE
-            for chunk in range(SIDE // 2):
-                for half in range(2):
-                    source[group, half, index * (SIDE // 2) + chunk] = part[
-                        chunk * depth : (chunk + 1) * depth, half * 128 : (half + 1) * 128
-                    ]
+        pair = all_ref[pl.ds(chip_at[group] * 2, 2)].reshape(width, all_ref.shape[2])
+        part = dot(pair, image_ref[...], NN)
+        depth = width // SIDE
+        for chunk in range(SIDE):
+            for half in range(2):
+                source[group, half, chunk] = part[
+                    chunk * depth : (chunk + 1) * depth, half * 128 : (half + 1) * 128
+                ]
         sent.extend(
             exchange(
                 2,
@@ -436,45 +442,51 @@
             chip = lax.rem(other // 2 + group, chips)
             wait_for(gram_ref.at[chip, other], gram_recv.at[group, other], (vtx, other))
 
-    own = pose
     up, down, across = [chip_at[g] * 2 + core for g in (1, 3, 2)]
-    send(sketch_ref, all_ref.at[own], recv_sem.at[0, own], peer[1], 0)
-    send(sketch_ref, all_ref.at[own], recv_sem.at[0, own], peer[3], 1)
-    send(sketch_ref, all_ref.at[own], recv_sem.at[0, own], sibling, 2)
-    all_ref[own] = sketch_ref[...]
-    other = sibling[1]
-    wait_for(all_ref.at[other], recv_sem.at[0, other], sibling)
+    up_peer, down_peer = peer[1], peer[3]
+
+    def send_half(slot, half, device, number):
+        send(half_of(slot, half), half_of(slot, half), recv_sem.at[half, slot], device, number)
+
+    def pass_on(slot, half, origin, targets, number):
+        wait_for(half_of(slot, half), recv_sem.at[half, slot], origin)
+        for index, device in enumerate(targets):
+            send_half(slot, half, device, number + index)
+
+    def from_sibling(group):
+        slot = chip_at[group] * 2 + 1 - core
+        for half in range(2):
+            wait_for(half_of(slot, half), recv_sem.at[half, slot], sibling)
+
+    send_half(pose, 0, up_peer, 0)
+    send_half(pose, 1, down_peer, 1)
+    for half in range(2):
+        send_half(pose, half, sibling, 2 + half)
+    from_sibling(0)
     start_sum(0)
+    send_half(pose, 1, up_peer, 4)
+    send_half(pose, 0, down_peer, 5)
+    pass_on(down, 0, down_peer, (up_peer, sibling), 6)
+    pass_on(up, 1, up_peer, (down_peer, sibling), 8)
     second_leg(0)
-    wait_for(all_ref.at[down], recv_sem.at[0, down], peer[3])
-    send(half_of(down, 0), half_of(down, 0), recv_sem.at[0, down], peer[1], 3)
-    send(all_ref.at[down], all_ref.at[down], recv_sem.at[0, down], sibling, 4)
-    wait_for(all_ref.at[up], recv_sem.at[0, up], peer[1])
-    send(half_of(up, 1), half_of(up, 1), recv_sem.at[1, up], peer[3], 5)
-    send(all_ref.at[up], all_ref.at[up], recv_sem.at[0, up], sibling, 6)
+    pass_on(down, 1, down_peer, (sibling,), 10)
+    pass_on(up, 0, up_peer, (sibling,), 11)
     third_leg(0)
     for group in (3, 1):
-        slot = chip_at[group] * 2 + 1 - core
-        wait_for(all_ref.at[slot], recv_sem.at[0, slot], sibling)
+        from_sibling(group)
         start_sum(group)
+    pass_on(across, 0, down_peer, (sibling,), 12)
+    pass_on(across, 1, up_peer, (sibling,), 13)
+    from_sibling(2)
+    start_sum(2)
     end_sum(0)
     gram_part(0)
-    second_leg(3)
-    second_leg(1)
-    wait_for(half_of(across, 0), recv_sem.at[0, across], peer[3])
-    send(half_of(across, 0), half_of(across, 0), recv_sem.at[0, across], sibling, 7)
-    wait_for(half_of(across, 1), recv_sem.at[1, across], peer[1])
-    send(half_of(across, 1), half_of(across, 1), recv_sem.at[1, across], sibling, 8)
-    slot = chip_at[2] * 2 + 1 - core
-    wait_for(half_of(slot, 0), recv_sem.at[0, slot], sibling)
-    wait_for(half_of(slot, 1), recv_sem.at[1, slot], sibling)
-    start_sum(2)
-    third_leg(3)
-    third_leg(1)
-    second_leg(2)
+    for group in (3, 1, 2):
+        second_leg(group)
+    for group in (3, 1, 2):
+        third_leg(group)
     end_sum(1)
     gram_part(1)
-    third_leg(2)
     end_sum(3)
     end_sum(2)
     gram_part(2)
@@ -496,6 +508,24 @@
             parts.append(jnp.zeros((height, width * (len(blocks) - 1 - index)), F32))
         rows.append(jnp.concatenate(parts, axis=1) if len(parts) > 1 else parts[0])
     return jnp.concatenate(rows, axis=0) if len(rows) > 1 else rows[0]
+
+
+def congruence(blocks, gram):
+    width = blocks[0].shape[1]
+    left = jnp.concatenate(
+        [
+            dot(block, gram[index * width : (index + 1) * width, :], NN, HIGHEST)
+            for index, block in enumerate(blocks)
+        ],
+        axis=0,
+    )
+    return jnp.concatenate(
+        [
+            dot(block, left[:, index * width : (index + 1) * width], NT, HIGHEST)
+            for index, block in enumerate(blocks)
+        ],
+        axis=0,
+    )
 
 
 def merge_kernel(rows_ref, product_ref, all_ref, basis_ref, coefficients_ref, joint_ref, space_ref):
@@ -528,7 +558,7 @@
         merged = turn if merged is None else dot(turn, merged, NN, HIGHEST)
         if pairs == 1:
             break
-        gram = dot(dot(turn, gram, NN, HIGHEST), turn, NT, HIGHEST)
+        gram = congruence(spaces, gram)
     merged = merged.astype(BF16)
     wide = merged.astype(F32)
     image = dot(wide, joint_ref[...], NN, HIGHEST)
@@ -573,7 +603,7 @@
         in_specs=[VMEM, SMEM, SMEM, VMEM],
         out_specs=(VMEM, VMEM),
         scratch_shapes=[pltpu.VMEM((rows // 4, poses), BF16), pltpu.VMEM((wide, poses), F32)],
-        compiler_params=params(24),
+        compiler_params=params(50),
         name="leaf",
     )(skin_weights, bone_ids, slot_mask, coeffs)
     gram = pl.pallas_call(
@@ -585,18 +615,15 @@
         compiler_params=params(8, collective_id=0, has_side_effects=True),
         name="gram_sum",
     )(part)
-    turn, sketch = pl.pallas_call(
+    turn = pl.pallas_call(
         turn_kernel,
-        out_shape=(
-            jax.ShapeDtypeStruct((RANK, poses), BF16),
-            jax.ShapeDtypeStruct((RANK, wide), BF16),
-        ),
-        in_specs=[VMEM, VMEM],
-        out_specs=(VMEM, VMEM),
+        out_shape=jax.ShapeDtypeStruct((RANK, poses), BF16),
+        in_specs=[VMEM],
+        out_specs=VMEM,
         scratch_shapes=[pltpu.VMEM((1, RANK, poses), F32)],
         compiler_params=params(12),
         name="turn",
-    )(gram, coeffs)
+    )(gram)
     sketches, product, joint_gram = pl.pallas_call(
         joint_kernel,
         out_shape=(
@@ -608,14 +635,14 @@
         out_specs=(VMEM, VMEM, VMEM),
         scratch_shapes=sum_scratch(2 * RANK, (shards // 2,))
         + [
-            pltpu.SemaphoreType.DMA((9,)),
+            pltpu.SemaphoreType.DMA((14,)),
             pltpu.SemaphoreType.DMA((2, shards)),
             pltpu.SemaphoreType.DMA((3, shards)),
             pltpu.SemaphoreType.DMA((3, shards)),
         ],
         compiler_params=params(20, collective_id=1, has_side_effects=True),
         name="joint",
-    )(sketch, image, turn)
+    )(coeffs, image, turn)
     basis, coefficients = pl.pallas_call(
         merge_kernel,
         out_shape=(

time: 125 us -> 120 us (0.960)
  local copies, waits for them, and re-layouts: 4.55 us -> 1.37 us
  Pallas kernels: 121 us -> 119 us
    unnamed x10 -> x8, local copies, waits for them, and re-layouts: 4.55 us -> 1.37 us
    pallas_call x1, Pallas kernels: 56.7 us -> 54.4 us  [per_device(): pl.pallas_call(joint_kernel, out_shape=(jax.ShapeDtypeStruct((shards, RAN...]
    pallas_call x1, Pallas kernels: 8.77 us -> 10.6 us  [per_device(): pl.pallas_call(leaf_kernel, out_shape=(jax.ShapeDtypeStruct((poses, poses...]
where the time goes in v3:
time: 120 us
  Pallas kernels  119 us (99%)
  local copies, waits for them, and re-layouts  1.37 us (1%)
    pallas_call x1, Pallas kernels, per_device(): pl.pallas_call(joint_kernel, out_shape=(jax.ShapeDtypeStruct((shards, RAN...  54.4 us
    pallas_call x1, Pallas kernels, per_device(): pl.pallas_call(gram_sum_kernel, out_shape=jax.ShapeDtypeStruct((poses, po...  29.9 us
    pallas_call x1, Pallas kernels, per_device(): pl.pallas_call(merge_kernel, out_shape=(jax.ShapeDtypeStruct((wide, RANK)...  16.7 us
    pallas_call x1, Pallas kernels, per_device(): pl.pallas_call(leaf_kernel, out_shape=(jax.ShapeDtypeStruct((poses, poses...  10.6 us
    pallas_call x1, Pallas kernels, per_device(): pl.pallas_call(project_kernel, out_shape=jax.ShapeDtypeStruct((rows, pose...  3.97 us
    pallas_call x1, Pallas kernels, per_device(): pl.pallas_call(turn_kernel, out_shape=jax.ShapeDtypeStruct((RANK, poses),...  3.11 us

profile of v3, /device:TPU:1, one launch (start us, length us, event | category | flops | bytes accessed | tf_op | source)
XLA Modules:
  0.0 120.0 jit_solution(5106492234529359549)
XLA Ops:
  0.0 0.0 copy-start.2
  0.0 0.7 copy-done.2
  0.7 0.0 copy-start.3
  0.7 0.7 copy-done.3
  1.4 0.0 copy-start.1
  1.4 10.6 %leaf.1 = (f32[256,256]{1,0:T(8,128)S(1)}, bf16[4096,256]{1,0:T(8,128)(2,1)S(1)}) custom-call(bf16[8192,128]{1,0:T(8,128)(2,1)} %skin_ref.3, s32[4,32]{1,0:T(4,128)S(1)} %bitcast.7, s32[4,32]{1,0:T(4,128)S(1)} %bitcast.9, bf16[4096,256]{1,0:T(8,128)(2,1)} %bitcast.4), custom_call_target="tpu_custom_call" | custom-call | tf_op jit(solution)/shard_map/leaf/pallas_call | solution.py:597
  11.9 29.9 %gram_sum.1.gram_ref = f32[256,256]{1,0:T(8,128)S(1)} custom-call(f32[256,256]{1,0:T(8,128)S(1)} %get-tuple-element.13.part_ref), custom_call_target="tpu_custom_call" | custom-call | tf_op jit(solution)/shard_map/gram_sum/pallas_call | solution.py:609
  41.8 3.1 %turn.1.turn_ref = bf16[64,256]{1,0:T(8,128)(2,1)S(1)} custom-call(f32[256,256]{1,0:T(8,128)S(1)} %gram_sum.1.gram_ref), custom_call_target="tpu_custom_call" | custom-call | tf_op jit(solution)/shard_map/turn/pallas_call | solution.py:618
  45.0 0.0 copy-done.1
  45.0 54.4 %joint.1 = (bf16[8,64,4096]{2,1,0:T(8,128)(2,1)S(1)}, f32[512,256]{1,0:T(8,128)S(1)}, f32[4,8,64,128]{3,2,1,0:T(8,128)S(1)}) custom-call(bf16[4096,256]{1,0:T(8,128)(2,1)S(1)} %bitcast.5, bf16[4096,256]{1,0:T(8,128)(2,1)S(1)} %get-tuple-element.12.image_ref, bf16[64,256]{1,0:T(8,128)(2,1)S(1)} %turn.1.turn_ref), custom_call_target="tpu_custom_call" | custom-call | tf_op jit(solution)/shard_map/joint/pallas_call | solution.py:627
  99.3 0.0 copy-start
  99.3 16.7 %merge.1 = (bf16[4096,64]{1,0:T(8,128)(2,1)S(1)}, bf16[64,256]{1,0:T(8,128)(2,1)S(1)}) custom-call(f32[4,8,64,128]{3,2,1,0:T(8,128)S(1)} %get-tuple-element.14.rows_ref, f32[512,256]{1,0:T(8,128)S(1)} %get-tuple-element.15.product_ref, bf16[512,4096]{1,0:T(8,128)(2,1)S(1)} %bitcast.6), custom_call_target="tpu_custom_call" | custom-call | tf_op jit(solution)/shard_map/merge/pallas_call | solution.py:646
  116.0 0.0 copy-done
  116.1 4.0 %project.1 = bf16[8192,256]{1,0:T(8,128)(2,1)} custom-call(s32[4,32]{1,0:T(4,128)S(1)} %bitcast.8, s32[4,32]{1,0:T(4,128)S(1)} %bitcast.10, bf16[8192,128]{1,0:T(8,128)(2,1)S(1)} %copy-done, bf16[4096,64]{1,0:T(8,128)(2,1)S(1)} %get-tuple-element.17.basis_ref, bf16[64,256]{1,0:T(8,128)(2,1)S(1)} %get-tuple-element.18.coefficients_ref), custom_call_target="tpu_custom_call" | custom-call | tf_op jit(solution)/shard_map/project/pallas_call | solution.py:662
Async XLA Ops:
  0.0 0.7 copy-start.2
  0.7 0.7 copy-start.3
  1.4 43.6 %copy-start.1 = (bf16[128,32,256]{2,1,0:T(8,128)(2,1)S(1)}, bf16[128,32,256]{2,1,0:T(8,128)(2,1)}, u32[]{:S(2)}) copy-start(bf16[128,32,256]{2,1,0:T(8,128)(2,1)} %param.7) | copy-start | bytes 6291460
  99.3 16.7 %copy-start = (bf16[8192,128]{1,0:T(8,128)(2,1)S(1)}, bf16[8192,128]{1,0:T(8,128)(2,1)}, u32[]{:S(2)}) copy-start(bf16[8192,128]{1,0:T(8,128)(2,1)} %skin_ref.3) | copy-start | bytes 6291460

commit v4 on v3

--- a/solution.py
+++ b/solution.py
@@ -132,6 +132,13 @@
         ).wait_recv()
 
 
+def total_of(parts):
+    value = parts[0].astype(F32)
+    for index in range(1, SIDE):
+        value += parts[index].astype(F32)
+    return value
+
+
 def vtx_sum(source, first, second, total, sems, place):
     z, y, pose = place
     outer, inner = ("y", "z"), ("z", "y")
@@ -143,17 +150,11 @@
         arrived(half, outer[half], lambda h, o: first.at[h, o], sems[0], sems[1], place)
         me = mine[outer[half]]
         first[half, me] = source[half, me]
-        value = first[half, 0]
-        for index in range(1, SIDE):
-            value += first[half, index]
-        second[half, mine[inner[half]]] = value
+        second[half, mine[inner[half]]] = total_of(first.at[half]).astype(second.dtype)
         sent += exchange_one(half, inner[half], second, sems[2], sems[3], place)
     for half in range(2):
         arrived(half, inner[half], lambda h, o: second.at[h, o], sems[2], sems[3], place)
-        value = second[half, 0]
-        for index in range(1, SIDE):
-            value += second[half, index]
-        total[half, mine[outer[half]]] = value
+        total[half, mine[outer[half]]] = total_of(second.at[half]).astype(total.dtype)
         sent += exchange_one(half, outer[half], total, sems[4], sems[5], place)
     for half in range(2):
         arrived(half, outer[half], lambda h, o: total.at[h, o], sems[4], sems[5], place)
@@ -186,7 +187,7 @@
         for chunk in range(SIDE):
             chunks_ref[half, chunk] = matrix_ref[
                 chunk * depth : (chunk + 1) * depth, half * 128 : (half + 1) * 128
-            ]
+            ].astype(chunks_ref.dtype)
 
 
 def from_chunks(chunks_ref, matrix_ref):
@@ -205,10 +206,15 @@
     from_chunks(total, gram_ref)
 
 
-def sum_scratch(rows, groups=()):
-    return [pltpu.VMEM((*groups, 2, SIDE, rows // SIDE, 128), F32)] * 4 + [
-        pltpu.SemaphoreType.DMA((*groups, 2, SIDE))
-    ] * 6
+def sum_scratch(rows, last, groups=()):
+    return [
+        pltpu.VMEM((*groups, 2, SIDE, rows // SIDE, 128), dtype) for dtype in (BF16, BF16, BF16, last)
+    ] + [pltpu.SemaphoreType.DMA((*groups, 2, SIDE))] * 6
+
+
+def reciprocal(value):
+    start = pl.reciprocal(value, approx=True)
+    return start * (2.0 - value * start)
 
 
 def inverse_factors(grams):
@@ -235,7 +241,7 @@
             for c in range(8):
                 pivot = jnp.broadcast_to(spread[c][0][c : c + 1, :], (8, 128))
                 pivots = jnp.where(sublane == c, pivot, pivots)
-                inverse = 1.0 / pivot
+                inverse = reciprocal(pivot)
                 lead = jnp.broadcast_to(own[p][c : c + 1, :], (8, 128)) * inverse
                 leads = [
                     jnp.broadcast_to(spread[d][0][c : c + 1, :], (8, 128)) * inverse
@@ -262,21 +268,18 @@
     return inverse_factors(grams)
 
 
+def scaled(gram):
+    diagonal = lax.broadcasted_iota(jnp.int32, gram.shape, 0) == lax.broadcasted_iota(
+        jnp.int32, gram.shape, 1
+    )
+    largest = jnp.max(jnp.max(jnp.where(diagonal, gram, 0.0), axis=0, keepdims=True), axis=1, keepdims=True)
+    return gram * (1.0 / largest)
+
+
 def top_spaces(grams, out_ref):
-    columns = []
-    scaled = []
-    for gram in grams:
-        size = gram.shape[0]
-        diagonal = lax.broadcasted_iota(jnp.int32, (size, size), 0) == lax.broadcasted_iota(
-            jnp.int32, (size, size), 1
-        )
-        largest = jnp.max(
-            jnp.max(jnp.where(diagonal, gram, 0.0), axis=0, keepdims=True), axis=1, keepdims=True
-        )
-        scaled.append(gram * (1.0 / largest))
-        columns.append(scaled[-1][:RANK, :])
+    columns = [gram[:RANK, :] for gram in grams]
     for sweep in range(SWEEPS - 1):
-        columns = [dot(value, gram, NN, HIGHEST) for value, gram in zip(columns, scaled)]
+        columns = [dot(value, gram, NN, HIGHEST) for value, gram in zip(columns, grams)]
     factors, squares = factors_of(columns)
     worst = None
     for n, (factor, value) in enumerate(zip(factors, columns)):
@@ -306,10 +309,10 @@
 
 
 def turn_kernel(gram_ref, turn_ref, space_ref):
-    turn_ref[...] = top_spaces([gram_ref[...]], space_ref)[0].astype(BF16)
-
-
-def joint_kernel(coeffs_ref, image_ref, turn_ref, all_ref, product_ref, gram_ref, *scratch):
+    turn_ref[...] = top_spaces([scaled(gram_ref[...])], space_ref)[0].astype(BF16)
+
+
+def joint_kernel(coeffs_ref, image_ref, turn_ref, all_ref, product_ref, own_ref, other_ref, *scratch):
     source, first, second, total = scratch[:4]
     sems = scratch[4:10]
     send_sem, recv_sem, gram_send, gram_recv = scratch[10:]
@@ -369,7 +372,7 @@
             for half in range(2):
                 source[group, half, chunk] = part[
                     chunk * depth : (chunk + 1) * depth, half * 128 : (half + 1) * 128
-                ]
+                ].astype(source.dtype)
         sent.extend(
             exchange(
                 2,
@@ -389,10 +392,7 @@
             )
             me = mine[outer[half]]
             first[group, half, me] = source[group, half, me]
-            value = first[group, half, 0]
-            for index in range(1, SIDE):
-                value += first[group, half, index]
-            second[group, half, mine[inner[half]]] = value
+            second[group, half, mine[inner[half]]] = total_of(first.at[group, half]).astype(second.dtype)
             sent.extend(
                 exchange_one(half, inner[half], second.at[group], sems[2].at[group], sems[3].at[group], place)
             )
@@ -402,10 +402,7 @@
             arrived(
                 half, inner[half], lambda h, o: second.at[group, h, o], sems[2].at[group], sems[3].at[group], place
             )
-            value = second[group, half, 0]
-            for index in range(1, SIDE):
-                value += second[group, half, index]
-            total[group, half, mine[outer[half]]] = value
+            total[group, half, mine[outer[half]]] = total_of(second.at[group, half]).astype(total.dtype)
             sent.extend(
                 exchange_one(half, outer[half], total.at[group], sems[4].at[group], sems[5].at[group], place)
             )
@@ -417,17 +414,23 @@
             )
         row = pl.multiple_of(chip_at[group] * width, width)
         for half in range(2):
-            product_ref[pl.ds(row, width), half * 128 : (half + 1) * 128] = total[group, half].reshape(width, 128)
+            product_ref[pl.ds(row, width), half * 128 : (half + 1) * 128] = (
+                total[group, half].astype(F32).reshape(width, 128)
+            )
+
+    def gram_block(group, row):
+        return own_ref.at[row] if group == 0 else other_ref.at[group - 1, row]
 
     def gram_part(group):
         row = pl.multiple_of(chip_at[group] * width, width)
-        gram_ref[chip_at[group], pose] = dot(
-            turn_ref[...].astype(F32), product_ref[pl.ds(row, width), :], NT, HIGHEST
+        block = gram_block(group, pose)
+        block[...] = dot(turn_ref[...].astype(F32), product_ref[pl.ds(row, width), :], NT, HIGHEST).astype(
+            block.dtype
         )
         for offset in range(1, poses):
             copy = pltpu.make_async_remote_copy(
-                src_ref=gram_ref.at[chip_at[group], pose],
-                dst_ref=gram_ref.at[chip_at[group], pose],
+                src_ref=block,
+                dst_ref=block,
                 send_sem=gram_send.at[group, offset],
                 recv_sem=gram_recv.at[group, pose],
                 device_id=(vtx, lax.rem(pose + offset, poses)),
@@ -439,8 +442,7 @@
     def gram_arrived(group):
         for offset in range(1, poses):
             other = lax.rem(pose + offset, poses)
-            chip = lax.rem(other // 2 + group, chips)
-            wait_for(gram_ref.at[chip, other], gram_recv.at[group, other], (vtx, other))
+            wait_for(gram_block(group, other), gram_recv.at[group, other], (vtx, other))
 
     up, down, across = [chip_at[g] * 2 + core for g in (1, 3, 2)]
     up_peer, down_peer = peer[1], peer[3]
@@ -528,25 +530,24 @@
     )
 
 
-def merge_kernel(rows_ref, product_ref, all_ref, basis_ref, coefficients_ref, joint_ref, space_ref):
+def merge_kernel(own_ref, other_ref, product_ref, all_ref, basis_ref, coefficients_ref, joint_ref, space_ref):
     width = 2 * RANK
-    chips = rows_ref.shape[0]
+    chips = own_ref.shape[0] // 2
     for chip in range(chips):
         for other in range(chips):
-            behind = (chip - other) % chips == 1
+            group = (other - chip) % chips
             for index in range(2):
-                if behind:
-                    continue
-                joint_ref[
-                    chip * width + index * RANK : chip * width + (index + 1) * RANK,
-                    other * width : (other + 1) * width,
-                ] = rows_ref[other, 2 * chip + index]
+                row = 2 * chip + index
+                if group < 3:
+                    joint_ref[row * RANK : (row + 1) * RANK, other * width : (other + 1) * width] = (
+                        own_ref[row] if group == 0 else other_ref[group - 1, row].astype(F32)
+                    )
     for chip in range(chips):
         other = (chip - 1) % chips
         joint_ref[chip * width : (chip + 1) * width, other * width : (other + 1) * width] = joint_ref[
             other * width : (other + 1) * width, chip * width : (chip + 1) * width
         ].T
-    gram = joint_ref[...]
+    gram = scaled(joint_ref[...])
     merged = None
     while True:
         pairs = gram.shape[0] // width
@@ -611,7 +612,7 @@
         out_shape=jax.ShapeDtypeStruct((poses, poses), F32),
         in_specs=[VMEM],
         out_specs=VMEM,
-        scratch_shapes=sum_scratch(poses),
+        scratch_shapes=sum_scratch(poses, F32),
         compiler_params=params(8, collective_id=0, has_side_effects=True),
         name="gram_sum",
     )(part)
@@ -624,16 +625,17 @@
         compiler_params=params(12),
         name="turn",
     )(gram)
-    sketches, product, joint_gram = pl.pallas_call(
+    sketches, product, own, others = pl.pallas_call(
         joint_kernel,
         out_shape=(
             jax.ShapeDtypeStruct((shards, RANK, wide), BF16),
             jax.ShapeDtypeStruct((joint, poses), F32),
-            jax.ShapeDtypeStruct((shards // 2, shards, RANK, 2 * RANK), F32),
+            jax.ShapeDtypeStruct((shards, RANK, 2 * RANK), F32),
+            jax.ShapeDtypeStruct((2, shards, RANK, 2 * RANK), BF16),
         ),
         in_specs=[VMEM, VMEM, VMEM],
-        out_specs=(VMEM, VMEM, VMEM),
-        scratch_shapes=sum_scratch(2 * RANK, (shards // 2,))
+        out_specs=(VMEM, VMEM, VMEM, VMEM),
+        scratch_shapes=sum_scratch(2 * RANK, BF16, (shards // 2,))
         + [
             pltpu.SemaphoreType.DMA((14,)),
             pltpu.SemaphoreType.DMA((2, shards)),
@@ -649,7 +651,7 @@
             jax.ShapeDtypeStruct((wide, RANK), BF16),
             jax.ShapeDtypeStruct((RANK, poses), BF16),
         ),
-        in_specs=[VMEM, VMEM, VMEM],
+        in_specs=[VMEM, VMEM, VMEM, VMEM],
         out_specs=(VMEM, VMEM),
         scratch_shapes=[
             pltpu.VMEM((joint, joint), F32),
@@ -657,7 +659,7 @@
         ],
         compiler_params=params(24),
         name="merge",
-    )(joint_gram, product, sketches.reshape(joint, wide))
+    )(own, others, product, sketches.reshape(joint, wide))
     step_rows = rows // 2
     return pl.pallas_call(
         project_kernel,

time: 120 us -> 117 us (0.975)
  Pallas kernels: 119 us -> 115 us
    pallas_call x1, Pallas kernels: 54.4 us -> 51 us  [per_device(): pl.pallas_call(joint_kernel, out_shape=(jax.ShapeDtypeStruct((shards, RAN...]
    pallas_call x1, Pallas kernels: 29.9 us -> 28 us  [per_device(): pl.pallas_call(gram_sum_kernel, out_shape=jax.ShapeDtypeStruct((poses, po...]
    pallas_call x1, Pallas kernels: 16.7 us -> 18.1 us  [per_device(): pl.pallas_call(merge_kernel, out_shape=(jax.ShapeDtypeStruct((wide, RANK)...]
where the time goes in v4:
time: 117 us; the launch traced here: 116 us
  Pallas kernels  115 us (98%)
  local copies, waits for them, and re-layouts  1.37 us (1%)
    pallas_call x1, Pallas kernels, per_device(): pl.pallas_call(joint_kernel, out_shape=(jax.ShapeDtypeStruct((shards, RAN...  51 us
    pallas_call x1, Pallas kernels, per_device(): pl.pallas_call(gram_sum_kernel, out_shape=jax.ShapeDtypeStruct((poses, po...  28 us
    pallas_call x1, Pallas kernels, per_device(): pl.pallas_call(merge_kernel, out_shape=(jax.ShapeDtypeStruct((wide, RANK)...  18.1 us
    pallas_call x1, Pallas kernels, per_device(): pl.pallas_call(leaf_kernel, out_shape=(jax.ShapeDtypeStruct((poses, poses...  10.6 us
    pallas_call x1, Pallas kernels, per_device(): pl.pallas_call(project_kernel, out_shape=jax.ShapeDtypeStruct((rows, pose...  3.97 us
    pallas_call x1, Pallas kernels, per_device(): pl.pallas_call(turn_kernel, out_shape=jax.ShapeDtypeStruct((RANK, poses),...  3.45 us

profile of v4, /device:TPU:1, one launch (start us, length us, event | category | flops | bytes accessed | tf_op | source)
XLA Modules:
  0.0 116.4 jit_solution(13598680994597244236)
XLA Ops:
  0.0 0.0 copy-start.2
  0.0 0.7 copy-done.2
  0.7 0.0 copy-start.3
  0.7 0.7 copy-done.3
  1.4 0.0 copy-start.1
  1.4 10.6 %leaf.1 = (f32[256,256]{1,0:T(8,128)S(1)}, bf16[4096,256]{1,0:T(8,128)(2,1)S(1)}) custom-call(bf16[8192,128]{1,0:T(8,128)(2,1)} %skin_ref.3, s32[4,32]{1,0:T(4,128)S(1)} %bitcast.7, s32[4,32]{1,0:T(4,128)S(1)} %bitcast.9, bf16[4096,256]{1,0:T(8,128)(2,1)} %bitcast.4), custom_call_target="tpu_custom_call" | custom-call | tf_op jit(solution)/shard_map/leaf/pallas_call | solution.py:598
  11.9 28.0 %gram_sum.1.gram_ref = f32[256,256]{1,0:T(8,128)S(1)} custom-call(f32[256,256]{1,0:T(8,128)S(1)} %get-tuple-element.14.part_ref), custom_call_target="tpu_custom_call" | custom-call | tf_op jit(solution)/shard_map/gram_sum/pallas_call | solution.py:610
  39.9 3.5 %turn.1.turn_ref = bf16[64,256]{1,0:T(8,128)(2,1)S(1)} custom-call(f32[256,256]{1,0:T(8,128)S(1)} %gram_sum.1.gram_ref), custom_call_target="tpu_custom_call" | custom-call | tf_op jit(solution)/shard_map/turn/pallas_call | solution.py:619
  43.4 0.0 copy-done.1
  43.4 51.0 %joint.1 = (bf16[8,64,4096]{2,1,0:T(8,128)(2,1)S(1)}, f32[512,256]{1,0:T(8,128)S(1)}, f32[8,64,128]{2,1,0:T(8,128)S(1)}, bf16[2,8,64,128]{3,2,1,0:T(8,128)(2,1)S(1)}) custom-call(bf16[4096,256]{1,0:T(8,128)(2,1)S(1)} %bitcast.5, bf16[4096,256]{1,0:T(8,128)(2,1)S(1)} %get-tuple-element.13.image_ref, bf16[64,256]{1,0:T(8,128)(2,1)S(1)} %turn.1.turn_ref), custom_call_target="tpu_custom_call" | custom-call | tf_op jit(solution)/shard_map/joint/pallas_call | solution.py:628
  94.3 0.0 copy-start
  94.3 18.1 %merge.1 = (bf16[4096,64]{1,0:T(8,128)(2,1)S(1)}, bf16[64,256]{1,0:T(8,128)(2,1)S(1)}) custom-call(f32[8,64,128]{2,1,0:T(8,128)S(1)} %get-tuple-element.15.own_ref, bf16[2,8,64,128]{3,2,1,0:T(8,128)(2,1)S(1)} %get-tuple-element.16.other_ref, f32[512,256]{1,0:T(8,128)S(1)} %get-tuple-element.17.product_ref, bf16[512,4096]{1,0:T(8,128)(2,1)S(1)} %bitcast.6), custom_call_target="tpu_custom_call" | custom-call | tf_op jit(solution)/shard_map/merge/pallas_call | solution.py:648
  112.5 0.0 copy-done
  112.5 4.0 %project.1 = bf16[8192,256]{1,0:T(8,128)(2,1)} custom-call(s32[4,32]{1,0:T(4,128)S(1)} %bitcast.8, s32[4,32]{1,0:T(4,128)S(1)} %bitcast.10, bf16[8192,128]{1,0:T(8,128)(2,1)S(1)} %copy-done, bf16[4096,64]{1,0:T(8,128)(2,1)S(1)} %get-tuple-element.19.basis_ref, bf16[64,256]{1,0:T(8,128)(2,1)S(1)} %get-tuple-element.20.coefficients_ref), custom_call_target="tpu_custom_call" | custom-call | tf_op jit(solution)/shard_map/project/pallas_call | solution.py:664
Async XLA Ops:
  0.0 0.7 copy-start.2
  0.7 0.7 copy-start.3
  1.4 42.0 %copy-start.1 = (bf16[128,32,256]{2,1,0:T(8,128)(2,1)S(1)}, bf16[128,32,256]{2,1,0:T(8,128)(2,1)}, u32[]{:S(2)}) copy-start(bf16[128,32,256]{2,1,0:T(8,128)(2,1)} %param.7) | copy-start | bytes 6291460
  94.3 18.1 %copy-start = (bf16[8192,128]{1,0:T(8,128)(2,1)S(1)}, bf16[8192,128]{1,0:T(8,128)(2,1)}, u32[]{:S(2)}) copy-start(bf16[8192,128]{1,0:T(8,128)(2,1)} %skin_ref.3) | copy-start | bytes 6291460

commit v5 on v4

--- a/solution.py
+++ b/solution.py
@@ -37,34 +37,38 @@
     return jnp.concatenate(parts, axis=0)
 
 
-def leaf_kernel(skin_ref, ids_ref, mask_ref, coeffs_ref, gram_ref, image_ref, slab_ref, sums_ref):
+def leaf_kernel(ids_ref, mask_ref, skin_ref, coeffs_ref, gram_ref, image_ref, slab_ref, sums_ref):
     slots, block_count = ids_ref.shape
-    block_rows = skin_ref.shape[0] // block_count
-    group = slab_ref.shape[0] // block_rows
-    sums_ref[...] = jnp.zeros_like(sums_ref)
-    gram_ref[...] = jnp.zeros_like(gram_ref)
-
-    def step(index, carry):
-        images = []
-        for inside in range(group):
-            block = index * group + inside
-            rows = skin_ref[pl.ds(pl.multiple_of(block * block_rows, block_rows), block_rows), :]
-            slab = dot(rows, chosen_rows(ids_ref, mask_ref, coeffs_ref, block), NN).astype(BF16)
-            slab_ref[inside * block_rows : (inside + 1) * block_rows, :] = slab
-            images.append(dot(rows, slab, TN))
-        gram_ref[...] += dot(slab_ref[...], slab_ref[...], TN)
-        for inside in range(group):
-            block = index * group + inside
-            for slot in range(slots):
-                place = pl.multiple_of(ids_ref[slot, block] * SHAPES, SHAPES)
-                values = images[inside][slot * SHAPES : (slot + 1) * SHAPES, :]
-                sums_ref[pl.ds(place, SHAPES), :] += jnp.where(
-                    mask_ref[slot, block] != 0, values, jnp.zeros_like(values)
-                )
-        return carry
-
-    lax.fori_loop(0, block_count // group, step, 0)
-    image_ref[...] = sums_ref[...].astype(BF16)
+    step, steps = pl.program_id(0), pl.num_programs(0)
+    group = block_count // steps
+    block_rows = skin_ref.shape[0] // group
+
+    @pl.when(step == 0)
+    def _():
+        sums_ref[...] = jnp.zeros_like(sums_ref)
+        gram_ref[...] = jnp.zeros_like(gram_ref)
+
+    images = []
+    for inside in range(group):
+        here = slice(inside * block_rows, (inside + 1) * block_rows)
+        rows = skin_ref[here, :]
+        chosen = chosen_rows(ids_ref, mask_ref, coeffs_ref, step * group + inside)
+        slab = dot(rows, chosen, NN).astype(BF16)
+        slab_ref[here, :] = slab
+        images.append(dot(rows, slab, TN))
+    gram_ref[...] += dot(slab_ref[...], slab_ref[...], TN)
+    for inside in range(group):
+        block = step * group + inside
+        for slot in range(slots):
+            place = pl.multiple_of(ids_ref[slot, block] * SHAPES, SHAPES)
+            values = images[inside][slot * SHAPES : (slot + 1) * SHAPES, :]
+            sums_ref[pl.ds(place, SHAPES), :] += jnp.where(
+                mask_ref[slot, block] != 0, values, jnp.zeros_like(values)
+            )
+
+    @pl.when(step == steps - 1)
+    def _():
+        image_ref[...] = sums_ref[...].astype(BF16)
 
 
 def my_place():
@@ -206,15 +210,10 @@
     from_chunks(total, gram_ref)
 
 
-def sum_scratch(rows, last, groups=()):
-    return [
-        pltpu.VMEM((*groups, 2, SIDE, rows // SIDE, 128), dtype) for dtype in (BF16, BF16, BF16, last)
-    ] + [pltpu.SemaphoreType.DMA((*groups, 2, SIDE))] * 6
-
-
-def reciprocal(value):
-    start = pl.reciprocal(value, approx=True)
-    return start * (2.0 - value * start)
+def sum_scratch(rows, travels, groups=()):
+    return [pltpu.VMEM((*groups, 2, SIDE, rows // SIDE, 128), travels)] * 4 + [
+        pltpu.SemaphoreType.DMA((*groups, 2, SIDE))
+    ] * 6
 
 
 def inverse_factors(grams):
@@ -241,7 +240,7 @@
             for c in range(8):
                 pivot = jnp.broadcast_to(spread[c][0][c : c + 1, :], (8, 128))
                 pivots = jnp.where(sublane == c, pivot, pivots)
-                inverse = reciprocal(pivot)
+                inverse = 1.0 / pivot
                 lead = jnp.broadcast_to(own[p][c : c + 1, :], (8, 128)) * inverse
                 leads = [
                     jnp.broadcast_to(spread[d][0][c : c + 1, :], (8, 128)) * inverse
@@ -268,12 +267,12 @@
     return inverse_factors(grams)
 
 
-def scaled(gram):
-    diagonal = lax.broadcasted_iota(jnp.int32, gram.shape, 0) == lax.broadcasted_iota(
-        jnp.int32, gram.shape, 1
+def scale_of(grams):
+    diagonal = lax.broadcasted_iota(jnp.int32, grams[0].shape, 0) == lax.broadcasted_iota(
+        jnp.int32, grams[0].shape, 1
     )
-    largest = jnp.max(jnp.max(jnp.where(diagonal, gram, 0.0), axis=0, keepdims=True), axis=1, keepdims=True)
-    return gram * (1.0 / largest)
+    largest = jnp.where(diagonal, functools.reduce(jnp.maximum, grams), 0.0)
+    return 1.0 / jnp.max(jnp.max(largest, axis=0, keepdims=True), axis=1, keepdims=True)
 
 
 def top_spaces(grams, out_ref):
@@ -309,7 +308,8 @@
 
 
 def turn_kernel(gram_ref, turn_ref, space_ref):
-    turn_ref[...] = top_spaces([scaled(gram_ref[...])], space_ref)[0].astype(BF16)
+    gram = gram_ref[...]
+    turn_ref[...] = top_spaces([gram * scale_of([gram])], space_ref)[0].astype(BF16)
 
 
 def joint_kernel(coeffs_ref, image_ref, turn_ref, all_ref, product_ref, own_ref, other_ref, *scratch):
@@ -547,19 +547,22 @@
         joint_ref[chip * width : (chip + 1) * width, other * width : (other + 1) * width] = joint_ref[
             other * width : (other + 1) * width, chip * width : (chip + 1) * width
         ].T
-    gram = scaled(joint_ref[...])
+    gram = joint_ref
+    blocks = [gram[n * width : (n + 1) * width, n * width : (n + 1) * width] for n in range(chips)]
+    scale = scale_of(blocks)
+    blocks = [block * scale for block in blocks]
     merged = None
     while True:
-        pairs = gram.shape[0] // width
-        spaces = top_spaces(
-            [gram[n * width : (n + 1) * width, n * width : (n + 1) * width] for n in range(pairs)],
-            space_ref,
-        )
+        spaces = top_spaces(blocks, space_ref)
         turn = block_diagonal(spaces)
         merged = turn if merged is None else dot(turn, merged, NN, HIGHEST)
-        if pairs == 1:
+        if len(spaces) == 1:
             break
-        gram = congruence(spaces, gram)
+        factor = scale if gram is joint_ref else 1.0
+        gram = congruence(spaces, gram) * factor
+        blocks = [
+            gram[n * width : (n + 1) * width, n * width : (n + 1) * width] for n in range(len(spaces) // 2)
+        ]
     merged = merged.astype(BF16)
     wide = merged.astype(F32)
     image = dot(wide, joint_ref[...], NN, HIGHEST)
@@ -601,12 +604,13 @@
             jax.ShapeDtypeStruct((poses, poses), F32),
             jax.ShapeDtypeStruct((wide, poses), BF16),
         ),
-        in_specs=[VMEM, SMEM, SMEM, VMEM],
+        grid=(4,),
+        in_specs=[SMEM, SMEM, pl.BlockSpec((rows // 4, depth), lambda i: (i, 0)), VMEM],
         out_specs=(VMEM, VMEM),
         scratch_shapes=[pltpu.VMEM((rows // 4, poses), BF16), pltpu.VMEM((wide, poses), F32)],
         compiler_params=params(50),
         name="leaf",
-    )(skin_weights, bone_ids, slot_mask, coeffs)
+    )(bone_ids, slot_mask, skin_weights, coeffs)
     gram = pl.pallas_call(
         gram_sum_kernel,
         out_shape=jax.ShapeDtypeStruct((poses, poses), F32),

time: 117 us -> 116 us (level)
    pallas_call x1, Pallas kernels: 28 us -> 29.9 us  [per_device(): pl.pallas_call(gram_sum_kernel, out_shape=jax.ShapeDtypeStruct((poses, po...]
    pallas_call x1, Pallas kernels: 18.1 us -> 16.5 us  [per_device(): pl.pallas_call(merge_kernel, out_shape=(jax.ShapeDtypeStruct((wide, RANK)...]
where the time goes in v5:
time: 116 us
  Pallas kernels  114 us (98%)
  local copies, waits for them, and re-layouts  1.37 us (1%)
    pallas_call x1, Pallas kernels, per_device(): pl.pallas_call(joint_kernel, out_shape=(jax.ShapeDtypeStruct((shards, RAN...  50.8 us
    pallas_call x1, Pallas kernels, per_device(): pl.pallas_call(gram_sum_kernel, out_shape=jax.ShapeDtypeStruct((poses, po...  29.9 us
    pallas_call x1, Pallas kernels, per_device(): pl.pallas_call(merge_kernel, out_shape=(jax.ShapeDtypeStruct((wide, RANK)...  16.5 us
    pallas_call x1, Pallas kernels, per_device(): pl.pallas_call(leaf_kernel, out_shape=(jax.ShapeDtypeStruct((poses, poses...  10.2 us
    pallas_call x1, Pallas kernels, per_device(): pl.pallas_call(project_kernel, out_shape=jax.ShapeDtypeStruct((rows, pose...  3.97 us
    pallas_call x1, Pallas kernels, per_device(): pl.pallas_call(turn_kernel, out_shape=jax.ShapeDtypeStruct((RANK, poses),...  3.11 us

profile of v5, /device:TPU:1, one launch (start us, length us, event | category | flops | bytes accessed | tf_op | source)
XLA Modules:
  0.0 115.9 jit_solution(6002007905510254978)
XLA Ops:
  0.0 0.0 copy-start.2
  0.0 0.7 copy-done.2
  0.7 0.0 copy-start.3
  0.7 0.7 copy-done.3
  1.4 0.0 copy-start.1
  1.4 10.2 %leaf.1 = (f32[256,256]{1,0:T(8,128)S(1)}, bf16[4096,256]{1,0:T(8,128)(2,1)S(1)}) custom-call(s32[4,32]{1,0:T(4,128)S(1)} %bitcast.7, s32[4,32]{1,0:T(4,128)S(1)} %bitcast.9, bf16[8192,128]{1,0:T(8,128)(2,1)} %skin_ref.3, bf16[4096,256]{1,0:T(8,128)(2,1)} %bitcast.4), custom_call_target="tpu_custom_call" | custom-call | tf_op jit(solution)/shard_map/leaf/pallas_call | solution.py:601
  11.6 29.9 %gram_sum.1.gram_ref = f32[256,256]{1,0:T(8,128)S(1)} custom-call(f32[256,256]{1,0:T(8,128)S(1)} %get-tuple-element.14.part_ref), custom_call_target="tpu_custom_call" | custom-call | tf_op jit(solution)/shard_map/gram_sum/pallas_call | solution.py:614
  41.5 3.1 %turn.1.turn_ref = bf16[64,256]{1,0:T(8,128)(2,1)S(1)} custom-call(f32[256,256]{1,0:T(8,128)S(1)} %gram_sum.1.gram_ref), custom_call_target="tpu_custom_call" | custom-call | tf_op jit(solution)/shard_map/turn/pallas_call | solution.py:623
  44.6 0.0 copy-done.1
  44.6 50.8 %joint.1 = (bf16[8,64,4096]{2,1,0:T(8,128)(2,1)S(1)}, f32[512,256]{1,0:T(8,128)S(1)}, f32[8,64,128]{2,1,0:T(8,128)S(1)}, bf16[2,8,64,128]{3,2,1,0:T(8,128)(2,1)S(1)}) custom-call(bf16[4096,256]{1,0:T(8,128)(2,1)S(1)} %bitcast.5, bf16[4096,256]{1,0:T(8,128)(2,1)S(1)} %get-tuple-element.13.image_ref, bf16[64,256]{1,0:T(8,128)(2,1)S(1)} %turn.1.turn_ref), custom_call_target="tpu_custom_call" | custom-call | tf_op jit(solution)/shard_map/joint/pallas_call | solution.py:632
  95.4 0.0 copy-start
  95.4 16.5 %merge.1 = (bf16[4096,64]{1,0:T(8,128)(2,1)S(1)}, bf16[64,256]{1,0:T(8,128)(2,1)S(1)}) custom-call(f32[8,64,128]{2,1,0:T(8,128)S(1)} %get-tuple-element.15.own_ref, bf16[2,8,64,128]{3,2,1,0:T(8,128)(2,1)S(1)} %get-tuple-element.16.other_ref, f32[512,256]{1,0:T(8,128)S(1)} %get-tuple-element.17.product_ref, bf16[512,4096]{1,0:T(8,128)(2,1)S(1)} %bitcast.6), custom_call_target="tpu_custom_call" | custom-call | tf_op jit(solution)/shard_map/merge/pallas_call | solution.py:652
  111.9 0.0 copy-done
  112.0 4.0 %project.1 = bf16[8192,256]{1,0:T(8,128)(2,1)} custom-call(s32[4,32]{1,0:T(4,128)S(1)} %bitcast.8, s32[4,32]{1,0:T(4,128)S(1)} %bitcast.10, bf16[8192,128]{1,0:T(8,128)(2,1)S(1)} %copy-done, bf16[4096,64]{1,0:T(8,128)(2,1)S(1)} %get-tuple-element.19.basis_ref, bf16[64,256]{1,0:T(8,128)(2,1)S(1)} %get-tuple-element.20.coefficients_ref), custom_call_target="tpu_custom_call" | custom-call | tf_op jit(solution)/shard_map/project/pallas_call | solution.py:668
Async XLA Ops:
  0.0 0.7 copy-start.2
  0.7 0.7 copy-start.3
  1.4 43.2 %copy-start.1 = (bf16[128,32,256]{2,1,0:T(8,128)(2,1)S(1)}, bf16[128,32,256]{2,1,0:T(8,128)(2,1)}, u32[]{:S(2)}) copy-start(bf16[128,32,256]{2,1,0:T(8,128)(2,1)} %param.7) | copy-start | bytes 6291460
  95.4 16.5 %copy-start = (bf16[8192,128]{1,0:T(8,128)(2,1)S(1)}, bf16[8192,128]{1,0:T(8,128)(2,1)}, u32[]{:S(2)}) copy-start(bf16[8192,128]{1,0:T(8,128)(2,1)} %skin_ref.3) | copy-start | bytes 6291460

commit v6 on v5

--- a/solution.py
+++ b/solution.py
@@ -604,10 +604,10 @@
             jax.ShapeDtypeStruct((poses, poses), F32),
             jax.ShapeDtypeStruct((wide, poses), BF16),
         ),
-        grid=(4,),
-        in_specs=[SMEM, SMEM, pl.BlockSpec((rows // 4, depth), lambda i: (i, 0)), VMEM],
+        grid=(2,),
+        in_specs=[SMEM, SMEM, pl.BlockSpec((rows // 2, depth), lambda i: (i, 0)), VMEM],
         out_specs=(VMEM, VMEM),
-        scratch_shapes=[pltpu.VMEM((rows // 4, poses), BF16), pltpu.VMEM((wide, poses), F32)],
+        scratch_shapes=[pltpu.VMEM((rows // 2, poses), BF16), pltpu.VMEM((wide, poses), F32)],
         compiler_params=params(50),
         name="leaf",
     )(bone_ids, slot_mask, skin_weights, coeffs)

time: 116 us -> 116 us (level)
  no operation moved by 1% of the time
where the time goes in v6:
time: 116 us; the launch traced here: 115 us
  Pallas kernels  114 us (98%)
  local copies, waits for them, and re-layouts  1.37 us (1%)
    pallas_call x1, Pallas kernels, per_device(): pl.pallas_call(joint_kernel, out_shape=(jax.ShapeDtypeStruct((shards, RAN...  50.6 us
    pallas_call x1, Pallas kernels, per_device(): pl.pallas_call(gram_sum_kernel, out_shape=jax.ShapeDtypeStruct((poses, po...  29.9 us
    pallas_call x1, Pallas kernels, per_device(): pl.pallas_call(merge_kernel, out_shape=(jax.ShapeDtypeStruct((wide, RANK)...  16.5 us
    pallas_call x1, Pallas kernels, per_device(): pl.pallas_call(leaf_kernel, out_shape=(jax.ShapeDtypeStruct((poses, poses...  9.89 us
    pallas_call x1, Pallas kernels, per_device(): pl.pallas_call(project_kernel, out_shape=jax.ShapeDtypeStruct((rows, pose...  3.97 us
    pallas_call x1, Pallas kernels, per_device(): pl.pallas_call(turn_kernel, out_shape=jax.ShapeDtypeStruct((RANK, poses),...  3.11 us

profile of v6, /device:TPU:1, one launch (start us, length us, event | category | flops | bytes accessed | tf_op | source)
XLA Modules:
  0.0 115.4 jit_solution(1432978565124775443)
XLA Ops:
  0.0 0.0 copy-start.2
  0.0 0.7 copy-done.2
  0.7 0.0 copy-start.3
  0.7 0.7 copy-done.3
  1.4 0.0 copy-start.1
  1.4 9.9 %leaf.1 = (f32[256,256]{1,0:T(8,128)S(1)}, bf16[4096,256]{1,0:T(8,128)(2,1)S(1)}) custom-call(s32[4,32]{1,0:T(4,128)S(1)} %bitcast.7, s32[4,32]{1,0:T(4,128)S(1)} %bitcast.9, bf16[8192,128]{1,0:T(8,128)(2,1)} %skin_ref.3, bf16[4096,256]{1,0:T(8,128)(2,1)} %bitcast.4), custom_call_target="tpu_custom_call" | custom-call | tf_op jit(solution)/shard_map/leaf/pallas_call | solution.py:601
  11.3 29.9 %gram_sum.1.gram_ref = f32[256,256]{1,0:T(8,128)S(1)} custom-call(f32[256,256]{1,0:T(8,128)S(1)} %get-tuple-element.14.part_ref), custom_call_target="tpu_custom_call" | custom-call | tf_op jit(solution)/shard_map/gram_sum/pallas_call | solution.py:614
  41.2 3.1 %turn.1.turn_ref = bf16[64,256]{1,0:T(8,128)(2,1)S(1)} custom-call(f32[256,256]{1,0:T(8,128)S(1)} %gram_sum.1.gram_ref), custom_call_target="tpu_custom_call" | custom-call | tf_op jit(solution)/shard_map/turn/pallas_call | solution.py:623
  44.3 0.0 copy-done.1
  44.3 50.6 %joint.1 = (bf16[8,64,4096]{2,1,0:T(8,128)(2,1)S(1)}, f32[512,256]{1,0:T(8,128)S(1)}, f32[8,64,128]{2,1,0:T(8,128)S(1)}, bf16[2,8,64,128]{3,2,1,0:T(8,128)(2,1)S(1)}) custom-call(bf16[4096,256]{1,0:T(8,128)(2,1)S(1)} %bitcast.5, bf16[4096,256]{1,0:T(8,128)(2,1)S(1)} %get-tuple-element.13.image_ref, bf16[64,256]{1,0:T(8,128)(2,1)S(1)} %turn.1.turn_ref), custom_call_target="tpu_custom_call" | custom-call | tf_op jit(solution)/shard_map/joint/pallas_call | solution.py:632
  94.9 0.0 copy-start
  94.9 16.5 %merge.1 = (bf16[4096,64]{1,0:T(8,128)(2,1)S(1)}, bf16[64,256]{1,0:T(8,128)(2,1)S(1)}) custom-call(f32[8,64,128]{2,1,0:T(8,128)S(1)} %get-tuple-element.15.own_ref, bf16[2,8,64,128]{3,2,1,0:T(8,128)(2,1)S(1)} %get-tuple-element.16.other_ref, f32[512,256]{1,0:T(8,128)S(1)} %get-tuple-element.17.product_ref, bf16[512,4096]{1,0:T(8,128)(2,1)S(1)} %bitcast.6), custom_call_target="tpu_custom_call" | custom-call | tf_op jit(solution)/shard_map/merge/pallas_call | solution.py:652
  111.4 0.0 copy-done
  111.4 4.0 %project.1 = bf16[8192,256]{1,0:T(8,128)(2,1)} custom-call(s32[4,32]{1,0:T(4,128)S(1)} %bitcast.8, s32[4,32]{1,0:T(4,128)S(1)} %bitcast.10, bf16[8192,128]{1,0:T(8,128)(2,1)S(1)} %copy-done, bf16[4096,64]{1,0:T(8,128)(2,1)S(1)} %get-tuple-element.19.basis_ref, bf16[64,256]{1,0:T(8,128)(2,1)S(1)} %get-tuple-element.20.coefficients_ref), custom_call_target="tpu_custom_call" | custom-call | tf_op jit(solution)/shard_map/project/pallas_call | solution.py:668
Async XLA Ops:
  0.0 0.7 copy-start.2
  0.7 0.7 copy-start.3
  1.4 42.9 %copy-start.1 = (bf16[128,32,256]{2,1,0:T(8,128)(2,1)S(1)}, bf16[128,32,256]{2,1,0:T(8,128)(2,1)}, u32[]{:S(2)}) copy-start(bf16[128,32,256]{2,1,0:T(8,128)(2,1)} %param.7) | copy-start | bytes 6291460
  94.9 16.5 %copy-start = (bf16[8192,128]{1,0:T(8,128)(2,1)S(1)}, bf16[8192,128]{1,0:T(8,128)(2,1)}, u32[]{:S(2)}) copy-start(bf16[8192,128]{1,0:T(8,128)(2,1)} %skin_ref.3) | copy-start | bytes 6291460
